TPU v7x, 256 devices: a whole 4x4x8 slice. The times are simulated.
256 devices in a mesh: req: 32 (over z_lo, x, core), tp: 8 (over y, z_hi).
Axes of the slice: x: 4, y: 4, z: 8 (z_hi: 2, z_lo: 4; z = z_hi * 4 + z_lo), core: 2. Of those that a mesh axis runs over, the one named last changes fastest.
Arguments:
- queries: bfloat16 [32768, 8192], P('req', 'tp'), may hold values from -6 to 6
- new_kv: bfloat16 [32768, 2048], P('req', 'tp'), may hold values from -6 to 6
- pool_kv: bfloat16 [512, 64, 2048], P(('req', 'tp')), may hold values from -6 to 6
- slot_request: int32 [64], P('req'), may hold values from 0 to 1, as said below
- prefix_ids: int32 [64, 16], P('req'), may hold values from 0 to 511, as said below
- prefix_count: int32 [64], P('req'), may hold values from 12 to 16
- block_row: int32 [512], replicated, may hold values from 0 to 511, as said below
Outputs:
- attended: bfloat16 [32768, 8192], P('req', 'tp')
Inputs may be any that keep to these rules, and one draw needn't show every extreme that they name: `slot_request`: within one index of req the 2 values never fall. `prefix_ids`: no block repeats within a request. The live prefix blocks of the 2 requests of one index of req, taken together, include at most 2 distinct blocks whose rows lie on the devices of any one index of req; some draw reaches 2. `block_row`: A permutation; row g lies on device g // 2 of the joined axes req+tp.
All inputs are finite; a program needn't handle non-finite values.
Results may differ from a plain program's by a relative error of at most 0.0049.
Values may be sent and summed in bfloat16 or wider, within the bound.
No kernel may reach another device: no remote copies, remote signals or barrier semaphores. Data moves between devices by JAX's collectives and lax.ppermute only.
A program may use at most 64 MiB of HBM per device.

v0:
```python
import math

import jax
import jax.numpy as jnp
from jax import lax
from jax.sharding import PartitionSpec as P

HD = 128
REQ_DEV = 2
PREF = 16
PB = 64


def lookup(indices, table_values):
    positions = jnp.arange(table_values.shape[0], dtype=jnp.int32)
    return jnp.sum(jnp.where(indices[..., None] == positions, table_values, 0), axis=-1)


def attend(queries, new_kv, prefix_kv, slot_request, prefix_count):
    slot_total = slot_request.shape[0]
    span_len = queries.shape[0] // slot_total
    head_count = queries.shape[1] // HD
    kv_heads = new_kv.shape[1] // (2 * HD)
    group_size = head_count // kv_heads
    score_scale = 1.0 / math.sqrt(HD)
    fresh_kv = new_kv.reshape(slot_total * span_len, kv_heads, 2, HD)
    cached = prefix_kv.reshape(REQ_DEV, PREF * PB, kv_heads, 2, HD)
    cached_live = (jnp.arange(PREF * PB, dtype=jnp.int32) // PB)[None, :] < prefix_count[:, None]
    token_owner = jnp.repeat(slot_request, span_len)
    pieces = []
    for slot_index in range(slot_total):
        owner_req = slot_request[slot_index]
        key_count = (slot_index + 1) * span_len
        key_index = jnp.arange(key_count, dtype=jnp.int32)
        query_index = slot_index * span_len + jnp.arange(span_len, dtype=jnp.int32)
        fresh_live = (token_owner[:key_count] == owner_req)[None, :] & (
            key_index[None, :] <= query_index[:, None]
        )
        prefix_live = jnp.broadcast_to(cached_live[owner_req][None, :], (span_len, PREF * PB))
        live_mask = jnp.concatenate([prefix_live, fresh_live], axis=1)
        key_values = jnp.concatenate([cached[owner_req], fresh_kv[:key_count]], axis=0)
        query_block = queries[slot_index * span_len : (slot_index + 1) * span_len].reshape(
            span_len, head_count, HD
        )

        def one_head(head_index):
            query_head = lax.dynamic_index_in_dim(query_block, head_index, 1, keepdims=False)
            head_pair = lax.dynamic_index_in_dim(
                key_values, head_index // group_size, 1, keepdims=False
            )
            scores = (
                jnp.einsum(
                    "nd,md->nm", query_head, head_pair[:, 0], preferred_element_type=jnp.float32
                )
                * score_scale
            )
            scores = jnp.where(live_mask, scores, -jnp.inf)
            row_max = jnp.max(scores, axis=1, keepdims=True)
            exponent = jnp.exp(scores - row_max)
            weights = (exponent / jnp.sum(exponent, axis=1, keepdims=True)).astype(jnp.bfloat16)
            return jnp.dot(weights, head_pair[:, 1], preferred_element_type=jnp.float32).astype(
                jnp.bfloat16
            )

        heads_out = lax.map(one_head, jnp.arange(head_count, dtype=jnp.int32))
        pieces.append(jnp.transpose(heads_out, (1, 0, 2)).reshape(span_len, head_count * HD))
    return jnp.concatenate(pieces, axis=0)


def on_device(queries, new_kv, pool_kv, slot_request, prefix_ids, prefix_count, block_row):
    tp_count = lax.axis_size("tp")
    pool_local = pool_kv.shape[0]
    head_width = pool_kv.shape[2] // tp_count
    split_heads = pool_kv.reshape(pool_local, PB, tp_count, head_width)
    regrouped = lax.all_to_all(split_heads, "tp", split_axis=2, concat_axis=0, tiled=True)
    group_rows = tp_count * pool_local
    group_store = regrouped.reshape(group_rows, PB * head_width)
    block_rows = lookup(prefix_ids, block_row)
    every_block = lax.all_gather(group_store, "req", axis=0, tiled=True)
    prefix_flat = jnp.take(every_block, block_rows.reshape(-1), axis=0)
    prefix_kv = prefix_flat.reshape(REQ_DEV, PREF * PB * head_width)
    return attend(queries, new_kv, prefix_kv, slot_request, prefix_count)


def solution(mesh):
    return jax.shard_map(
        on_device,
        mesh=mesh,
        in_specs=(
            P("req", "tp"),
            P("req", "tp"),
            P(("req", "tp"), None, None),
            P("req"),
            P("req", None),
            P("req"),
            P(),
        ),
        out_specs=P("req", "tp"),
        check_vma=False,
    )
```

profile of v0, /device:TPU:1, one launch (start us, length us, event | category | flops | bytes accessed | tf_op | source)
XLA Modules:
  0.0 271.9 jit_solution(7528235486019368585)
XLA Ops:
  7.8 25.7 %all_to_all.15 = bf16[2,64,8,256]{3,1,0,2:T(8,128)(2,1)S(1)} all-to-all(bf16[2,64,8,256]{3,1,0,2:T(8,128)(2,1)S(1)} %bitcast.109), channel_id=1, replica_groups=mesh['req'=32,'tp'=8] {'tp'}, dimensions={2} | all-to-all | bytes 1048576 | tf_op jit(solution)/shard_map/all_to_all | solution.py:75
  39.2 1.7 fusion.24
  47.1 88.6 %all-gather.2.cloned.1.call-done = bf16[512,16384]{1,0:T(8,128)(2,1)} async-done(((bf16[16,16384]{1,0:T(8,128)(2,1)}), bf16[512,16384]{1,0:T(8,128)(2,1)}) %all-gather.2.cloned.1.call-update) | async-done | bytes 16777232 | tf_op jit(solution)/shard_map/all_gather | solution.py:79
  135.7 10.0 %gather_fusion = bf16[32,16384]{1,0:T(8,128)(2,1)S(1)} fusion(bf16[512,16384]{1,0:T(8,128)(2,1)} %all-gather.2.cloned.1.call-done, s32[1024]{0:T(1024)S(1)} %pad_clamp_fusion), kind=kCustom, calls=%fused_computation | custom fusion | bytes 2097280 | tf_op jit(solution)/shard_map/jit(_take)/gather | solution.py:80
  147.3 8.5 %broadcast_select_fusion = bf16[2,1024,1,2,128]{4,3,1,0,2:T(2,128)(2,1)S(1)} fusion(bf16[2,1024,1,2,128]{4,3,1,0,2:T(2,128)(2,1)} %gather.7, pred[2,1024]{1,0:T(4,128)(4,1)S(1)} %broadcast_in_dim.71), kind=kLoop, calls=%fused_computation.33 | loop fusion | flops 524288 | bytes 2099200 | tf_op jit(solution)/shard_map/jit(_take)/select_n | solution.py:80
  157.7 2.1 pad_maximum_fusion.1
  162.6 51.5 %while.21 = (s32[]{:T(128)}, bf16[8,512,128]{2,1,0:T(8,128)(2,1)}, s32[8]{0:T(128)S(1)}, bf16[512,8,128]{0,2,1:T(8,128)(2,1)}, bf16[2048,1,2,128]{3,0,2,1:T(8,12...) while((s32[]{:T(128)}, bf16[8,512,128]{2,1,0:T(8,128)(2,1)}, ...), condition=%wide.region_8.9_spmd, body=%wide.region_5.8_spmd.sunk | while | flops 545324032 | bytes 14953103 | solution.py:65
  164.9 1.9 fusion.37
  171.3 1.9 fusion.37
  177.7 1.9 fusion.37
  184.2 1.9 fusion.37
  190.6 1.9 fusion.37
  197.1 1.9 fusion.37
  203.5 1.9 fusion.37
  209.9 1.9 fusion.37
  215.3 46.7 %while.20 = (s32[]{:T(128)}, bf16[8,512,128]{2,1,0:T(8,128)(2,1)S(1)}, s32[8]{0:T(128)S(1)}, bf16[512,8,128]{0,2,1:T(8,128)(2,1)}, bf16[1536,1,2,128]{3,0,2,1:T(...) while((s32[]{:T(128)}, bf16[8,512,128]{2,1,0:T(8,128)(2,1)S(1)}, ...), condition=%wide.region_4.5_spmd, body=%wide.region_1.0_spmd.sunk | while | flops 409009152 | bytes 11282579 | solution.py:65
  218.3 1.7 fusion.34
  224.1 1.7 fusion.34
  229.9 1.7 fusion.34
  235.7 1.7 fusion.34
  241.5 1.7 fusion.34
  247.3 1.7 fusion.34
  253.2 1.7 fusion.34
  259.0 1.7 fusion.34
  (100 shorter events, 58.3 us)
Async XLA Ops:
  6.5 28.0 %copy-start.2 = (s32[2]{0:T(128)S(1)}, s32[2]{0:T(128)}, u32[]{:S(2)}) copy-start(s32[2]{0:T(128)} %param.14) | copy-start | bytes 28
  6.5 32.0 %copy-start.3 = (s32[2,16]{1,0:T(2,128)S(1)}, s32[2,16]{1,0:T(2,128)}, u32[]{:S(2)}) copy-start(s32[2,16]{1,0:T(2,128)} %param.15) | copy-start | bytes 388
  6.5 32.0 %copy-start.1 = (s32[512]{0:T(512)S(1)}, s32[512]{0:T(512)}, u32[]{:S(2)}) copy-start(s32[512]{0:T(512)} %param.17) | copy-start | bytes 6148
  6.5 32.4 %copy-start = (bf16[1024,256]{1,0:T(8,128)(2,1)S(1)}, bf16[1024,256]{1,0:T(8,128)(2,1)}, u32[]{:S(2)}) copy-start(bf16[1024,256]{1,0:T(8,128)(2,1)} %param.12) | copy-start | bytes 1572868
  6.5 129.2 %all-gather.2.cloned.1.call-start = ((), (), s32[]{:S(2)}) async-start(), calls=%async_computation.1 | async-start | bytes 17301504 | tf_op jit(solution)/shard_map/all_gather | solution.py:79
  39.2 5.3 %copy-start.4 = (s32[2]{0:T(128)S(1)}, s32[2]{0:T(128)}, u32[]{:S(2)}) copy-start(s32[2]{0:T(128)} %param.16) | copy-start | bytes 28
Sparse Core Ops, SparseCore 0:
  34.7 100.9 all-gather.1
where the time goes:
time: 273 us; the launch traced here: 272 us
  waiting for transfers between devices  88.6 us (32%)
  matrix products  47.5 us (17%)
  local copies, waits for them, and re-layouts  36.7 us (13%)
  loops' own time  30.5 us (11%)
  blocking collectives  25.7 us (9%)
  other arithmetic  25.5 us (9%)
  between operations  17.5 us (6%)
    all_gather x1, waiting for transfers between devices, on_device(): every_block = lax.all_gather(group_store, 'req', axis=0, tiled=True)  88.6 us
    another operation x2, loops' own time, attend(): heads_out = lax.map(one_head, jnp.arange(head_count, dtype=jnp.int32))  30.5 us
    dot_general x16, matrix products, one_head(): jnp.einsum('nd,md->nm', query_head, head_pair[:, 0], preferred_element_ty...  29 us
    all_to_all x1, blocking collectives, on_device(): lax.all_to_all(split_heads, 'tp', split_axis=2, concat_axis=0, tiled=True)  25.7 us
    dot_general x16, matrix products, one_head(): jnp.dot(weights, head_pair[:, 1], preferred_element_type=jnp.float32)  18.5 us
    gather x2, local copies, waits for them, and re-layouts, on_device(): prefix_flat = jnp.take(every_block, block_rows.reshape(-1), axis=0)  11.6 us
    reduce_sum x16, other arithmetic, one_head(): jnp.sum(exponent, axis=1, keepdims=True)  10.3 us
    dynamic_slice x16, local copies, waits for them, and re-layouts, attend(): heads_out = lax.map(one_head, jnp.arange(head_count, dtype=jnp.int32))  9.99 us
  transfers between devices with their start and end apart: 1, of which 1 were waited for; matrix products, arithmetic and copies ran while one was open for 3% of the time, Pallas kernels for 0%

commit v1 on v0

v1 whole, which is shorter than its diff:
```python
import functools
import math

import jax
import jax.numpy as jnp
from jax import lax
from jax.experimental import pallas as pl
from jax.experimental.pallas import tpu as pltpu
from jax.sharding import PartitionSpec as P

HD = 128
REQ_DEV = 2
PREF = 16
PB = 64
SLOT_CAP = 2
MIN_LIVE = 12
ROW_TILE = 256
EXP_SCALE = math.log2(math.e) / math.sqrt(HD)
MASKED = -1e30


def pick_blocks(wanted, group_store):
    count = wanted.shape[0]

    def kernel(wanted_ref, store_ref, out_ref, sems):
        def copy(i):
            return pltpu.make_async_copy(store_ref.at[wanted_ref[i]], out_ref.at[i], sems.at[i])

        def start(i, carry):
            copy(i).start()
            return carry

        def finish(i, carry):
            copy(i).wait()
            return carry

        lax.fori_loop(0, count, start, 0)
        lax.fori_loop(0, count, finish, 0)

    return pl.pallas_call(
        kernel,
        grid_spec=pltpu.PrefetchScalarGridSpec(
            num_scalar_prefetch=1,
            grid=(1,),
            in_specs=[pl.BlockSpec(memory_space=pl.ANY)],
            out_specs=pl.BlockSpec(memory_space=pl.ANY),
            scratch_shapes=[pltpu.SemaphoreType.DMA((count,))],
        ),
        out_shape=jax.ShapeDtypeStruct((count,) + group_store.shape[1:], group_store.dtype),
        name="pick_blocks",
    )(wanted, group_store)


def scores_of(query_tile, keys):
    return lax.dot_general(
        query_tile, keys, (((1,), (1,)), ((), ())), preferred_element_type=jnp.float32
    )


def fresh_attention(queries, new_kv, slot_request):
    rows, width = queries.shape
    heads = width // HD
    span = rows // slot_request.shape[0]

    def kernel(owner_ref, q_ref, kv_ref, acc_ref, stat_ref, v_ext):
        @pl.when(pl.program_id(0) == 0)
        def _():
            v_ext[:, :HD] = kv_ref[:, HD:]
            v_ext[:, HD:] = jnp.ones((rows, HD), v_ext.dtype)

        same = owner_ref[0] == owner_ref[1]
        lane = lax.broadcasted_iota(jnp.int32, (ROW_TILE, HD), 1)
        for first in range(0, rows, ROW_TILE):
            last = first + ROW_TILE
            s = scores_of(q_ref[first:last, :], kv_ref[:last, :HD])
            key = lax.broadcasted_iota(jnp.int32, s.shape, 1)
            row = first + lax.broadcasted_iota(jnp.int32, s.shape, 0)
            own = (first // span) * span
            lowest = jnp.where(same, 0, own)
            s = jnp.where((key <= row) & (key >= lowest), s, MASKED)
            top = jnp.max(s, axis=1, keepdims=True)
            p = jnp.exp2((s - top) * EXP_SCALE).astype(jnp.bfloat16)
            o = jnp.dot(p, v_ext[:last, :], preferred_element_type=jnp.float32)
            acc_ref[first:last, :] = o[:, :HD]
            stat_ref[first:last, :] = jnp.where(lane < HD // 2, top, o[:, HD:])

    return pl.pallas_call(
        kernel,
        grid_spec=pltpu.PrefetchScalarGridSpec(
            num_scalar_prefetch=1,
            grid=(heads,),
            in_specs=[
                pl.BlockSpec((rows, HD), lambda h, owner: (0, h)),
                pl.BlockSpec((rows, 2 * HD), lambda h, owner: (0, 0)),
            ],
            out_specs=[
                pl.BlockSpec((rows, HD), lambda h, owner: (0, h)),
                pl.BlockSpec((rows, HD), lambda h, owner: (0, h)),
            ],
            scratch_shapes=[pltpu.VMEM((rows, 2 * HD), jnp.bfloat16)],
        ),
        out_shape=[
            jax.ShapeDtypeStruct((rows, width), jnp.float32),
            jax.ShapeDtypeStruct((rows, width), jnp.float32),
        ],
        compiler_params=pltpu.CompilerParams(vmem_limit_bytes=48 * 1024 * 1024),
        cost_estimate=pl.CostEstimate(
            flops=4 * rows * rows * width, bytes_accessed=12 * rows * width, transcendentals=rows * rows * heads
        ),
        name="fresh_attention",
    )(slot_request, queries, new_kv)


def prefix_attention(queries, received, acc, stat, slot_request, places, prefix_count):
    rows, width = queries.shape
    heads = width // HD
    slots = slot_request.shape[0]
    span = rows // slots
    keys = PREF * PB
    sure = MIN_LIVE * PB

    def kernel(owner_ref, place_ref, count_ref, q_ref, recv_ref, acc_ref, stat_ref, out_ref, k_scr, v_scr, sems):
        def copies(r, p):
            place = place_ref[r * PREF + p]
            dst = pl.ds(pl.multiple_of(p * PB, PB), PB)
            return (
                pltpu.make_async_copy(
                    recv_ref.at[place, :, pl.ds(0, HD)], k_scr.at[r, dst, :], sems.at[r, p, 0]
                ),
                pltpu.make_async_copy(
                    recv_ref.at[place, :, pl.ds(HD, HD)], v_scr.at[r, dst, pl.ds(0, HD)], sems.at[r, p, 1]
                ),
            )

        @pl.when(pl.program_id(0) == 0)
        def _():
            for r in range(REQ_DEV):
                def start(p, carry):
                    for c in copies(r, p):
                        c.start()
                    return carry

                lax.fori_loop(0, PREF, start, 0)
            v_scr[:, :, HD:] = jnp.ones((REQ_DEV, keys, HD), v_scr.dtype)
            for r in range(REQ_DEV):
                def finish(p, carry):
                    for c in copies(r, p):
                        c.wait()
                    return carry

                lax.fori_loop(0, PREF, finish, 0)

        for slot in range(slots):
            owner = owner_ref[slot]
            live = count_ref[owner] * PB
            for first in range(slot * span, (slot + 1) * span, ROW_TILE):
                tile = pl.ds(first, ROW_TILE)
                q = q_ref[tile, :]
                s = scores_of(q, k_scr[owner])
                key = sure + lax.broadcasted_iota(jnp.int32, (ROW_TILE, keys - sure), 1)
                s = jnp.concatenate([s[:, :sure], jnp.where(key < live, s[:, sure:], MASKED)], axis=1)
                old_top = stat_ref[tile, 0:1]
                top = jnp.maximum(old_top, jnp.max(s, axis=1, keepdims=True))
                p = jnp.exp2((s - top) * EXP_SCALE).astype(jnp.bfloat16)
                o = jnp.dot(p, v_scr[owner], preferred_element_type=jnp.float32)
                keep = jnp.exp2((old_top - top) * EXP_SCALE)
                total = stat_ref[tile, HD - 1 : HD] * keep + o[:, HD:]
                out_ref[tile, :] = ((acc_ref[tile, :] * keep + o[:, :HD]) / total).astype(out_ref.dtype)

    column = pl.BlockSpec((rows, HD), lambda h, *_: (0, h))
    return pl.pallas_call(
        kernel,
        grid_spec=pltpu.PrefetchScalarGridSpec(
            num_scalar_prefetch=3,
            grid=(heads,),
            in_specs=[column, pl.BlockSpec(memory_space=pl.ANY), column, column],
            out_specs=column,
            scratch_shapes=[
                pltpu.VMEM((REQ_DEV, keys, HD), jnp.bfloat16),
                pltpu.VMEM((REQ_DEV, keys, 2 * HD), jnp.bfloat16),
                pltpu.SemaphoreType.DMA((REQ_DEV, PREF, 2)),
            ],
        ),
        out_shape=jax.ShapeDtypeStruct((rows, width), jnp.bfloat16),
        compiler_params=pltpu.CompilerParams(vmem_limit_bytes=48 * 1024 * 1024),
        cost_estimate=pl.CostEstimate(
            flops=4 * rows * keys * width, bytes_accessed=12 * rows * width, transcendentals=rows * keys * heads
        ),
        name="prefix_attention",
    )(slot_request, places, prefix_count, queries, received, acc, stat)


def wanted_blocks(prefix_ids, prefix_count, block_row, groups, group_rows):
    known = jnp.arange(block_row.shape[0], dtype=jnp.int32)
    rows = jnp.sum(jnp.where(prefix_ids.reshape(-1)[:, None] == known, block_row, 0), axis=-1)
    live = (jnp.arange(PREF, dtype=jnp.int32)[None, :] < prefix_count[:, None]).reshape(-1)
    group, within = rows // group_rows, rows % group_rows
    member = live[None, :] & (group[None, :] == jnp.arange(groups, dtype=jnp.int32)[:, None])
    low = jnp.min(jnp.where(member, within[None, :], group_rows), axis=1)
    high = jnp.max(jnp.where(member, within[None, :], 0), axis=1)
    wanted = jnp.stack([jnp.minimum(low, high), high], axis=1)
    is_high = jnp.any(member & (within[None, :] > low[:, None]), axis=0)
    places = jnp.where(live, SLOT_CAP * group + is_high.astype(jnp.int32), 0)
    return wanted, places


def on_device(queries, new_kv, pool_kv, slot_request, prefix_ids, prefix_count, block_row):
    tp_count = lax.axis_size("tp")
    groups = lax.axis_size("req")
    pool_local = pool_kv.shape[0]
    head_width = pool_kv.shape[2] // tp_count
    group_rows = tp_count * pool_local
    wanted, places = wanted_blocks(prefix_ids, prefix_count, block_row, groups, group_rows)
    asked = lax.all_to_all(wanted, "req", split_axis=0, concat_axis=0, tiled=True)
    by_head = pool_kv.reshape(pool_local, PB, tp_count, head_width).transpose(2, 0, 1, 3)
    group_store = lax.all_to_all(by_head, "tp", split_axis=0, concat_axis=0, tiled=True)
    group_store = group_store.reshape(group_rows, PB, head_width)
    to_send = pick_blocks(asked.reshape(-1), group_store)
    received = lax.all_to_all(to_send, "req", split_axis=0, concat_axis=0, tiled=True)
    acc, stat = fresh_attention(queries, new_kv, slot_request)
    return prefix_attention(queries, received, acc, stat, slot_request, places, prefix_count)


def solution(mesh):
    return jax.shard_map(
        on_device,
        mesh=mesh,
        in_specs=(
            P("req", "tp"),
            P("req", "tp"),
            P(("req", "tp"), None, None),
            P("req"),
            P("req", None),
            P("req"),
            P(),
        ),
        out_specs=P("req", "tp"),
        check_vma=False,
    )
```

time: 273 us -> 189 us (0.69)
  Pallas kernels: 0 us -> 102 us
  matrix products: 47.5 us -> 0 us
  waiting for transfers between devices: 88.6 us -> 48.7 us
  loops' own time: 30.5 us -> 0 us
  local copies, waits for them, and re-layouts: 36.7 us -> 8.51 us
  starting transfers between devices: 0.03 us -> 26.2 us
  blocking collectives: 25.7 us -> 0 us
  other arithmetic: 25.5 us -> 2.44 us
  between operations: 17.5 us -> 0.1 us
    pallas_call x0 -> x3, Pallas kernels: none -> 102 us  [the longest x1 65.9 us: pick_blocks(): pl.pallas_call(kernel, grid_spec=pltpu.PrefetchScalarGridSpec(num_scalar_...]
    all_gather x1 -> x0, waiting for transfers between devices: 88.6 us -> none  [on_device(): every_block = lax.all_gather(group_store, 'req', axis=0, tiled=True)]
    all_to_all x0 -> x3, waiting for transfers between devices: none -> 48.7 us  [the longest x1 29.8 us: on_device(): lax.all_to_all(to_send, 'req', split_axis=0, concat_axis=0, tiled=True)]
    dot_general x32 -> x0, matrix products: 47.5 us -> none  [the longest x16 29 us: one_head(): jnp.einsum('nd,md->nm', query_head, head_pair[:, 0], preferred_element_ty...]
    another operation x2 -> x0, loops' own time: 30.5 us -> none  [attend(): heads_out = lax.map(one_head, jnp.arange(head_count, dtype=jnp.int32))]
    all_to_all x0 -> x3, starting transfers between devices: none -> 26.2 us  [the longest x1 10 us: on_device(): lax.all_to_all(wanted, 'req', split_axis=0, concat_axis=0, tiled=True)]
    all_to_all x1 -> x0, blocking collectives: 25.7 us -> none  [on_device(): lax.all_to_all(split_heads, 'tp', split_axis=2, concat_axis=0, tiled=True)]
    dynamic_slice x20 -> x0, local copies, waits for them, and re-layouts: 12 us -> none  [the longest x16 9.99 us: attend(): heads_out = lax.map(one_head, jnp.arange(head_count, dtype=jnp.int32))]
  transfers between devices with their start and end apart: 1 -> 3, of which waited for: 1 -> 3; matrix products, arithmetic and copies ran while one was open for 3% -> 2% of each run, Pallas kernels for 0% -> 9%
where the time goes in v1:
time: 189 us; the launch traced here: 188 us
  Pallas kernels  102 us (54%)
  waiting for transfers between devices  48.7 us (26%)
  starting transfers between devices  26.2 us (14%)
  local copies, waits for them, and re-layouts  8.51 us (5%)
  other arithmetic  2.44 us (1%)
    pallas_call x1, Pallas kernels, pick_blocks(): pl.pallas_call(kernel, grid_spec=pltpu.PrefetchScalarGridSpec(num_scalar_...  65.9 us
    all_to_all x1, waiting for transfers between devices, on_device(): lax.all_to_all(to_send, 'req', split_axis=0, concat_axis=0, tiled=True)  29.8 us
    pallas_call x1, Pallas kernels, prefix_attention(): pl.pallas_call(kernel, grid_spec=pltpu.PrefetchScalarGridSpec(num_scalar_...  19.7 us
    pallas_call x1, Pallas kernels, fresh_attention(): pl.pallas_call(kernel, grid_spec=pltpu.PrefetchScalarGridSpec(num_scalar_...  16.7 us
    all_to_all x1, waiting for transfers between devices, on_device(): lax.all_to_all(by_head, 'tp', split_axis=0, concat_axis=0, tiled=True)  13.5 us
    all_to_all x1, starting transfers between devices, on_device(): lax.all_to_all(wanted, 'req', split_axis=0, concat_axis=0, tiled=True)  10 us
    all_to_all x1, starting transfers between devices, on_device(): lax.all_to_all(by_head, 'tp', split_axis=0, concat_axis=0, tiled=True)  8.12 us
    all_to_all x1, starting transfers between devices, on_device(): lax.all_to_all(to_send, 'req', split_axis=0, concat_axis=0, tiled=True)  8.09 us
  transfers between devices with their start and end apart: 3, of which 3 were waited for; matrix products, arithmetic and copies ran while one was open for 2% of the time, Pallas kernels for 9%

profile of v1, /device:TPU:1, one launch (start us, length us, event | category | flops | bytes accessed | tf_op | source)
XLA Modules:
  0.0 188.2 jit_solution(10939712450777872077)
XLA Ops:
  0.0 0.8 eq.30
  0.8 0.7 iota_compare_fusion.2
  1.5 0.1 lt.30
  1.6 0.9 select_reduce_fusion
  2.5 0.1 select_reduce_fusion.1
  2.6 0.7 copy.14
  3.3 10.0 %all-to-all-start = ((s32[32,1,2]{2,1,0:T(1,128)}), s32[32,1,2]{2,1,0:T(1,128)S(1)}, u32[]{:S(2)}, u32[]{:S(2)}) async-start(s32[32,1,2]{2,1,0:T(1,128)} %copy.14), calls=%async_computation | async-start | bytes 32768 | tf_op jit(solution)/shard_map/all_to_all | solution.py:214
  13.3 1.9 %copy.18 = bf16[2,8,8,8,256]{4,3,1,0,2:T(8,128)(2,1)} copy(bf16[2,8,8,8,256]{4,3,2,1,0:T(8,128)(2,1)} %bitcast.15) | data formatting | bytes 1048576 | tf_op jit(solution)/shard_map/reshape | solution.py:215
  15.2 5.4 %all-to-all-done = s32[32,1,2]{2,1,0:T(1,128)S(1)} async-done(((s32[32,1,2]{2,1,0:T(1,128)}), s32[32,1,2]{2,1,0:T(1,128)S(1)}, u32[]{:S(2)}, u32[]{:S(2)}) %all-to-all-start) | async-done | bytes 288 | tf_op jit(solution)/shard_map/all_to_all | solution.py:214
  20.6 8.1 %all-to-all-start.1 = ((bf16[8,2,64,256]{3,2,1,0:T(8,128)(2,1)}), bf16[8,2,64,256]{3,2,1,0:T(8,128)(2,1)S(1)}, u32[]{:S(2)}, u32[]{:S(2)}) async-start(bf16[8,2,64,256]{3,2,1,0:T(8,128)(2,1)} %bitcast.13), calls=%async_computation.1 | async-start | bytes 1048576 | tf_op jit(solution)/shard_map/all_to_all | solution.py:216
  28.7 0.5 broadcast.80
  29.3 0.6 reduce.3
  29.9 0.6 reshape.73.wanted_ref
  30.5 13.5 %all-to-all-done.1 = bf16[8,2,64,256]{3,2,1,0:T(8,128)(2,1)S(1)} async-done(((bf16[8,2,64,256]{3,2,1,0:T(8,128)(2,1)}), bf16[8,2,64,256]{3,2,1,0:T(8,128)(2,1)S(1)}, u32[]{:S(2)}, u32[]{:S(2)}) %all-to-all-start.1) | async-done | bytes 524320 | tf_op jit(solution)/shard_map/all_to_all | solution.py:216
  44.0 0.8 copy-done.5
  44.8 65.9 %pick_blocks.1 = bf16[64,64,256]{2,1,0:T(8,128)(2,1)} custom-call(s32[64]{0:T(128)} %reshape.73.wanted_ref, bf16[16,64,256]{2,1,0:T(8,128)(2,1)} %bitcast.14), custom_call_target="tpu_custom_call" | custom-call | tf_op jit(solution)/shard_map/pick_blocks/pallas_call | solution.py:40
  110.6 0.0 copy-start.2
  110.7 8.1 %all-to-all-start.2 = ((bf16[64,64,256]{2,1,0:T(8,128)(2,1)}), bf16[64,64,256]{2,1,0:T(8,128)(2,1)S(1)}, u32[]{:S(2)}, u32[]{:S(2)}) async-start(bf16[64,64,256]{2,1,0:T(8,128)(2,1)} %pick_blocks.1), calls=%async_computation.2 | async-start | bytes 4194304 | tf_op jit(solution)/shard_map/all_to_all | solution.py:219
  118.8 0.1 fusion.2
  118.9 1.6 copy-done
  120.5 16.7 %fresh_attention.1 = (f32[1024,1024]{1,0:T(8,128)}, f32[1024,1024]{1,0:T(8,128)}) custom-call(s32[2]{0:T(128)S(1)} %copy-done.3, bf16[1024,1024]{1,0:T(8,128)(2,1)S(1)} %copy-done, bf16[1024,256]{1,0:T(8,128)(2,1)S(1)} %copy-done.2), custom_call_target="tpu_custom_call" | custom-call | flops 4294967296 | bytes 12582912 | tf_op jit(solution)/shard_map/fresh_attention/pallas_call | solution.py:87
  137.1 29.8 %all-to-all-done.2.recv_ref = bf16[64,64,256]{2,1,0:T(8,128)(2,1)S(1)} async-done(((bf16[64,64,256]{2,1,0:T(8,128)(2,1)}), bf16[64,64,256]{2,1,0:T(8,128)(2,1)S(1)}, u32[]{:S(2)}, u32[]{:S(2)}) %all-to-all-start.2) | async-done | bytes 2097184 | tf_op jit(solution)/shard_map/all_to_all | solution.py:219
  166.9 1.6 copy-done.1
  168.5 19.7 %prefix_attention.1 = bf16[1024,1024]{1,0:T(8,128)(2,1)} custom-call(s32[2]{0:T(128)S(1)} %copy-done.3, s32[32]{0:T(128)S(1)} %add_select_fusion.place_ref, s32[2]{0:T(128)S(1)} %copy-done.4, bf16[1024,1024]{1,0:T(8,128)(2,1)S(1)} %copy-done.1, bf16[64,64,256]{2,1,0:T(8,128)(2,1)S(1)} %all-to-all-done.2.recv_ref, f32[1024,1024]{1,0:T(8,128)} %get-tuple-element.7.acc_ref, ...), custom_call_target="tpu_custom_call" | custom-call | flops 4294967296 | bytes 12582912 | tf_op jit(solution)/shard_map/prefix_attention/pallas_call | solution.py:171
  (12 shorter events, 0.1 us)
Async XLA Ops:
  3.3 17.3 %all-to-all-start = ((s32[32,1,2]{2,1,0:T(1,128)}), s32[32,1,2]{2,1,0:T(1,128)S(1)}, u32[]{:S(2)}, u32[]{:S(2)}) async-start(s32[32,1,2]{2,1,0:T(1,128)} %copy.14), calls=%async_computation | async-start | bytes 32768 | tf_op jit(solution)/shard_map/all_to_all | solution.py:214
  20.6 23.3 %all-to-all-start.1 = ((bf16[8,2,64,256]{3,2,1,0:T(8,128)(2,1)}), bf16[8,2,64,256]{3,2,1,0:T(8,128)(2,1)S(1)}, u32[]{:S(2)}, u32[]{:S(2)}) async-start(bf16[8,2,64,256]{3,2,1,0:T(8,128)(2,1)} %bitcast.13), calls=%async_computation.1 | async-start | bytes 1048576 | tf_op jit(solution)/shard_map/all_to_all | solution.py:216
  44.0 0.8 copy-start.5
  110.6 8.2 %copy-start.2 = (bf16[1024,256]{1,0:T(8,128)(2,1)S(1)}, bf16[1024,256]{1,0:T(8,128)(2,1)}, u32[]{:S(2)}) copy-start(bf16[1024,256]{1,0:T(8,128)(2,1)} %kv_ref.1) | copy-start | bytes 1572868
  110.6 8.2 %copy-start.3 = (s32[2]{0:T(128)S(1)}, s32[2]{0:T(128)}, u32[]{:S(2)}) copy-start(s32[2]{0:T(128)} %owner_ref.3) | copy-start | bytes 28
  110.7 56.2 %all-to-all-start.2 = ((bf16[64,64,256]{2,1,0:T(8,128)(2,1)}), bf16[64,64,256]{2,1,0:T(8,128)(2,1)S(1)}, u32[]{:S(2)}, u32[]{:S(2)}) async-start(bf16[64,64,256]{2,1,0:T(8,128)(2,1)} %pick_blocks.1), calls=%async_computation.2 | async-start | bytes 4194304 | tf_op jit(solution)/shard_map/all_to_all | solution.py:219
  118.9 1.6 copy-start
  120.5 46.4 %copy-start.4 = (s32[2]{0:T(128)S(1)}, s32[2]{0:T(128)}, u32[]{:S(2)}) copy-start(s32[2]{0:T(128)} %count_ref.1) | copy-start | bytes 28
  166.9 1.6 copy-start.1

commit v2 on v1

--- a/solution.py
+++ b/solution.py
@@ -14,41 +14,34 @@
 PB = 64
 SLOT_CAP = 2
 MIN_LIVE = 12
+PICK_STEP = 16
 ROW_TILE = 256
 EXP_SCALE = math.log2(math.e) / math.sqrt(HD)
 MASKED = -1e30
 
 
-def pick_blocks(wanted, group_store):
-    count = wanted.shape[0]
-
-    def kernel(wanted_ref, store_ref, out_ref, sems):
-        def copy(i):
-            return pltpu.make_async_copy(store_ref.at[wanted_ref[i]], out_ref.at[i], sems.at[i])
-
-        def start(i, carry):
-            copy(i).start()
-            return carry
-
-        def finish(i, carry):
-            copy(i).wait()
-            return carry
-
-        lax.fori_loop(0, count, start, 0)
-        lax.fori_loop(0, count, finish, 0)
+def pick_blocks(wanted, me, group_store):
+    groups = wanted.shape[0] // SLOT_CAP
+    block_shape = group_store.shape[1:]
+
+    def kernel(wanted_ref, me_ref, store_ref, out_ref):
+        first = pl.program_id(0) * PICK_STEP
+        for i in range(PICK_STEP):
+            for j in range(SLOT_CAP):
+                at = ((first + i) ^ me_ref[0]) * SLOT_CAP + j
+                out_ref[SLOT_CAP * i + j] = store_ref[wanted_ref[at]]
 
     return pl.pallas_call(
         kernel,
         grid_spec=pltpu.PrefetchScalarGridSpec(
-            num_scalar_prefetch=1,
-            grid=(1,),
-            in_specs=[pl.BlockSpec(memory_space=pl.ANY)],
-            out_specs=pl.BlockSpec(memory_space=pl.ANY),
-            scratch_shapes=[pltpu.SemaphoreType.DMA((count,))],
-        ),
-        out_shape=jax.ShapeDtypeStruct((count,) + group_store.shape[1:], group_store.dtype),
+            num_scalar_prefetch=2,
+            grid=(groups // PICK_STEP,),
+            in_specs=[pl.BlockSpec(group_store.shape, lambda i, *_: (0, 0, 0))],
+            out_specs=pl.BlockSpec((SLOT_CAP * PICK_STEP,) + block_shape, lambda i, *_: (i, 0, 0)),
+        ),
+        out_shape=jax.ShapeDtypeStruct((SLOT_CAP * groups,) + block_shape, group_store.dtype),
         name="pick_blocks",
-    )(wanted, group_store)
+    )(wanted, me, group_store)
 
 
 def scores_of(query_tile, keys):
@@ -190,33 +183,49 @@
     )(slot_request, places, prefix_count, queries, received, acc, stat)
 
 
-def wanted_blocks(prefix_ids, prefix_count, block_row, groups, group_rows):
+def used_rows(prefix_ids, prefix_count, block_row):
     known = jnp.arange(block_row.shape[0], dtype=jnp.int32)
-    rows = jnp.sum(jnp.where(prefix_ids.reshape(-1)[:, None] == known, block_row, 0), axis=-1)
+    ids = prefix_ids.reshape(-1)
+    rows = jnp.sum(jnp.where(ids[:, None] == known, block_row, 0), axis=-1)
     live = (jnp.arange(PREF, dtype=jnp.int32)[None, :] < prefix_count[:, None]).reshape(-1)
-    group, within = rows // group_rows, rows % group_rows
-    member = live[None, :] & (group[None, :] == jnp.arange(groups, dtype=jnp.int32)[:, None])
-    low = jnp.min(jnp.where(member, within[None, :], group_rows), axis=1)
-    high = jnp.max(jnp.where(member, within[None, :], 0), axis=1)
-    wanted = jnp.stack([jnp.minimum(low, high), high], axis=1)
-    is_high = jnp.any(member & (within[None, :] > low[:, None]), axis=0)
-    places = jnp.where(live, SLOT_CAP * group + is_high.astype(jnp.int32), 0)
-    return wanted, places
+    return jnp.where(live, rows, -1)
+
+
+def share_over_req(values):
+    groups = lax.axis_size("req")
+    known = values[None, :]
+    for steps in ((1,), (2, 4, 6), (8, 16, 24)):
+        parts = [lax.ppermute(known, "req", [(d, d ^ step) for d in range(groups)]) for step in steps]
+        known = jnp.concatenate([known] + parts, axis=0)
+    return known
+
+
+def low_high(rows, first_row, group_rows):
+    within = rows - first_row
+    member = (within >= 0) & (within < group_rows)
+    low = jnp.min(jnp.where(member, within, group_rows), axis=-1)
+    high = jnp.max(jnp.where(member, within, 0), axis=-1)
+    return jnp.minimum(low, high), high
 
 
 def on_device(queries, new_kv, pool_kv, slot_request, prefix_ids, prefix_count, block_row):
     tp_count = lax.axis_size("tp")
     groups = lax.axis_size("req")
+    me = lax.axis_index("req").astype(jnp.int32)
     pool_local = pool_kv.shape[0]
     head_width = pool_kv.shape[2] // tp_count
     group_rows = tp_count * pool_local
-    wanted, places = wanted_blocks(prefix_ids, prefix_count, block_row, groups, group_rows)
-    asked = lax.all_to_all(wanted, "req", split_axis=0, concat_axis=0, tiled=True)
+    rows = used_rows(prefix_ids, prefix_count, block_row)
+    low, high = low_high(share_over_req(rows), me * group_rows, group_rows)
+    wanted = jnp.stack([low, high], axis=1).reshape(-1)
     by_head = pool_kv.reshape(pool_local, PB, tp_count, head_width).transpose(2, 0, 1, 3)
     group_store = lax.all_to_all(by_head, "tp", split_axis=0, concat_axis=0, tiled=True)
     group_store = group_store.reshape(group_rows, PB, head_width)
-    to_send = pick_blocks(asked.reshape(-1), group_store)
+    to_send = pick_blocks(wanted, me[None], group_store)
     received = lax.all_to_all(to_send, "req", split_axis=0, concat_axis=0, tiled=True)
+    same_group = rows[:, None] // group_rows == rows[None, :] // group_rows
+    is_high = jnp.any(same_group & (rows[None, :] < rows[:, None]) & (rows[None, :] >= 0), axis=1)
+    places = jnp.where(rows >= 0, SLOT_CAP * (rows // group_rows) + is_high.astype(jnp.int32), 0)
     acc, stat = fresh_attention(queries, new_kv, slot_request)
     return prefix_attention(queries, received, acc, stat, slot_request, places, prefix_count)
 

time: 189 us -> 114 us (0.60)
  Pallas kernels: 102 us -> 40.1 us
  waiting for transfers between devices: 48.7 us -> 35.6 us
  starting transfers between devices: 26.2 us -> 30.4 us
    pallas_call x1, Pallas kernels: 65.9 us -> 3.11 us  [pick_blocks(): pl.pallas_call(kernel, grid_spec=pltpu.PrefetchScalarGridSpec(num_scalar_...]
    all_to_all x1, waiting for transfers between devices: 13.5 us -> 0.01 us  [on_device(): lax.all_to_all(by_head, 'tp', split_axis=0, concat_axis=0, tiled=True)]
    all_to_all x1 -> x0, starting transfers between devices: 10 us -> none  [on_device(): lax.all_to_all(wanted, 'req', split_axis=0, concat_axis=0, tiled=True)]
    ppermute x0 -> x7, starting transfers between devices: none -> 7.92 us  [share_over_req(): lax.ppermute(known, 'req', [(d, d ^ step) for d in range(groups)])]
    ppermute x0 -> x7, waiting for transfers between devices: none -> 6.01 us  [share_over_req(): lax.ppermute(known, 'req', [(d, d ^ step) for d in range(groups)])]
    all_to_all x1 -> x0, waiting for transfers between devices: 5.42 us -> none  [on_device(): lax.all_to_all(wanted, 'req', split_axis=0, concat_axis=0, tiled=True)]
    all_to_all x1, starting transfers between devices: 8.12 us -> 11.6 us  [on_device(): lax.all_to_all(by_head, 'tp', split_axis=0, concat_axis=0, tiled=True)]
    all_to_all x1, starting transfers between devices: 8.09 us -> 10.8 us  [on_device(): lax.all_to_all(to_send, 'req', split_axis=0, concat_axis=0, tiled=True)]
  transfers between devices with their start and end apart: 3 -> 9, of which waited for: 3 -> 6; matrix products, arithmetic and copies ran while one was open for 2% -> 1% of each run, Pallas kernels for 9% -> 15%
where the time goes in v2:
time: 114 us
  Pallas kernels  40.1 us (35%)
  waiting for transfers between devices  35.6 us (31%)
  starting transfers between devices  30.4 us (27%)
  local copies, waits for them, and re-layouts  6.95 us (6%)
    all_to_all x1, waiting for transfers between devices, on_device(): lax.all_to_all(to_send, 'req', split_axis=0, concat_axis=0, tiled=True)  29.6 us
    pallas_call x1, Pallas kernels, prefix_attention(): pl.pallas_call(kernel, grid_spec=pltpu.PrefetchScalarGridSpec(num_scalar_...  20.4 us
    pallas_call x1, Pallas kernels, fresh_attention(): pl.pallas_call(kernel, grid_spec=pltpu.PrefetchScalarGridSpec(num_scalar_...  16.7 us
    all_to_all x1, starting transfers between devices, on_device(): lax.all_to_all(by_head, 'tp', split_axis=0, concat_axis=0, tiled=True)  11.6 us
    all_to_all x1, starting transfers between devices, on_device(): lax.all_to_all(to_send, 'req', split_axis=0, concat_axis=0, tiled=True)  10.8 us
    ppermute x7, starting transfers between devices, share_over_req(): lax.ppermute(known, 'req', [(d, d ^ step) for d in range(groups)])  7.92 us
    ppermute x7, waiting for transfers between devices, share_over_req(): lax.ppermute(known, 'req', [(d, d ^ step) for d in range(groups)])  6.01 us
    unnamed x16, local copies, waits for them, and re-layouts  3.99 us
  transfers between devices with their start and end apart: 9, of which 6 were waited for; matrix products, arithmetic and copies ran while one was open for 1% of the time, Pallas kernels for 15%

profile of v2, /device:TPU:1, one launch (start us, length us, event | category | flops | bytes accessed | tf_op | source)
XLA Modules:
  0.0 113.8 jit_solution(8435955059510213011)
XLA Ops:
  0.0 1.9 %copy.16 = bf16[2,8,8,8,256]{4,3,1,0,2:T(8,128)(2,1)} copy(bf16[2,8,8,8,256]{4,3,2,1,0:T(8,128)(2,1)} %bitcast.16) | data formatting | bytes 1048576 | tf_op jit(solution)/shard_map/reshape | solution.py:221
  1.9 11.6 %all-to-all-start = ((bf16[8,2,64,256]{3,2,1,0:T(8,128)(2,1)}), bf16[8,2,64,256]{3,2,1,0:T(8,128)(2,1)S(1)}, u32[]{:S(2)}, u32[]{:S(2)}) async-start(bf16[8,2,64,256]{3,2,1,0:T(8,128)(2,1)} %bitcast.14), calls=%async_computation | async-start | bytes 1048576 | tf_op jit(solution)/shard_map/all_to_all | solution.py:222
  13.8 0.2 select_reduce_fusion
  14.0 1.0 collective-permute-start
  15.1 0.8 collective-permute-done
  15.9 2.5 %collective-permute-start.3 = (s32[2,32]{1,0:T(2,128)S(1)}, s32[2,32]{1,0:T(2,128)S(1)}, u32[]{:S(2)}, u32[]{:S(2)}) collective-permute-start(s32[2,32]{1,0:T(2,128)S(1)} %pad_add_fusion), channel_id=1, source_target_pairs={{0,48},{8,56},{16,32},{24,40},{32,16},{40,24},{48,0},{56,8},{64,11... | collective-permute-start | bytes 776 | tf_op jit(solution)/shard_map/ppermute | solution.py:198
  18.4 0.5 collective-permute-start.2
  18.9 0.3 collective-permute-start.1
  19.2 0.7 collective-permute-done.3
  19.8 2.8 %collective-permute-done.2 = s32[2,32]{1,0:T(2,128)S(1)} collective-permute-done((s32[2,32]{1,0:T(2,128)S(1)}, s32[2,32]{1,0:T(2,128)S(1)}, u32[]{:S(2)}, u32[]{:S(2)}) %collective-permute-start.2) | collective-permute-done | bytes 288 | tf_op jit(solution)/shard_map/ppermute | solution.py:198
  22.6 1.7 %collective-permute-start.6 = (s32[8,32]{1,0:T(8,128)S(1)}, s32[8,32]{1,0:T(8,128)S(1)}, u32[]{:S(2)}, u32[]{:S(2)}) collective-permute-start(s32[8,32]{1,0:T(8,128)S(1)} %concatenate.12), channel_id=1, source_target_pairs={{0,192},{8,200},{16,208},{24,216},{32,224},{40,232},{48,240},{56,2... | collective-permute-start | bytes 3080 | tf_op jit(solution)/shard_map/ppermute | solution.py:198
  24.4 1.9 %collective-permute-start.4 = (s32[8,32]{1,0:T(8,128)S(1)}, s32[8,32]{1,0:T(8,128)S(1)}, u32[]{:S(2)}, u32[]{:S(2)}) collective-permute-start(s32[8,32]{1,0:T(8,128)S(1)} %concatenate.12), channel_id=1, source_target_pairs={{0,64},{8,72},{16,80},{24,88},{32,96},{40,104},{48,112},{56,120},{... | collective-permute-start | bytes 3080 | tf_op jit(solution)/shard_map/ppermute | solution.py:198
  26.3 1.0 collective-permute-done.6
  27.3 0.7 collective-permute-done.5
  28.3 0.7 reshape.157.wanted_ref
  28.9 0.8 copy-done.5
  29.7 3.1 %pick_blocks.1 = bf16[64,64,256]{2,1,0:T(8,128)(2,1)} custom-call(s32[64]{0:T(128)} %reshape.157.wanted_ref, s32[1]{0:T(128)} %bitcast.3.me_ref, bf16[16,64,256]{2,1,0:T(8,128)(2,1)} %bitcast.15), custom_call_target="tpu_custom_call" | custom-call | tf_op jit(solution)/shard_map/pick_blocks/pallas_call | solution.py:34
  32.8 10.8 %all-to-all-start.1 = ((bf16[64,64,256]{2,1,0:T(8,128)(2,1)}), bf16[64,64,256]{2,1,0:T(8,128)(2,1)S(1)}, u32[]{:S(2)}, u32[]{:S(2)}) async-start(bf16[64,64,256]{2,1,0:T(8,128)(2,1)} %pick_blocks.1), calls=%async_computation.1 | async-start | bytes 4194304 | tf_op jit(solution)/shard_map/all_to_all | solution.py:225
  43.8 0.2 and_reduce_fusion
  44.0 1.6 %copy-done = bf16[1024,1024]{1,0:T(8,128)(2,1)S(1)} copy-done((bf16[1024,1024]{1,0:T(8,128)(2,1)S(1)}, bf16[1024,1024]{1,0:T(8,128)(2,1)}, u32[]{:S(2)}) %copy-start) | copy-done | bytes 2097176
  45.6 16.7 %fresh_attention.1 = (f32[1024,1024]{1,0:T(8,128)}, f32[1024,1024]{1,0:T(8,128)}) custom-call(s32[2]{0:T(128)S(1)} %copy-done.3, bf16[1024,1024]{1,0:T(8,128)(2,1)S(1)} %copy-done, bf16[1024,256]{1,0:T(8,128)(2,1)S(1)} %copy-done.2), custom_call_target="tpu_custom_call" | custom-call | flops 4294967296 | bytes 12582912 | tf_op jit(solution)/shard_map/fresh_attention/pallas_call | solution.py:80
  62.3 29.6 %all-to-all-done.1.recv_ref = bf16[64,64,256]{2,1,0:T(8,128)(2,1)S(1)} async-done(((bf16[64,64,256]{2,1,0:T(8,128)(2,1)}), bf16[64,64,256]{2,1,0:T(8,128)(2,1)S(1)}, u32[]{:S(2)}, u32[]{:S(2)}) %all-to-all-start.1) | async-done | bytes 2097184 | tf_op jit(solution)/shard_map/all_to_all | solution.py:225
  91.8 1.6 %copy-done.1 = bf16[1024,1024]{1,0:T(8,128)(2,1)S(1)} copy-done((bf16[1024,1024]{1,0:T(8,128)(2,1)S(1)}, bf16[1024,1024]{1,0:T(8,128)(2,1)}, u32[]{:S(2)}) %copy-start.1) | copy-done | bytes 2097176
  93.4 20.4 %prefix_attention.1 = bf16[1024,1024]{1,0:T(8,128)(2,1)} custom-call(s32[2]{0:T(128)S(1)} %copy-done.3, s32[32]{0:T(128)S(1)} %add_select_fusion.place_ref, s32[2]{0:T(128)S(1)} %copy-done.4, bf16[1024,1024]{1,0:T(8,128)(2,1)S(1)} %copy-done.1, bf16[64,64,256]{2,1,0:T(8,128)(2,1)S(1)} %all-to-all-done.1.recv_ref, f32[1024,1024]{1,0:T(8,128)} %get-tuple-element.7.acc_ref, ...), custom_call_target="tpu_custom_call" | custom-call | flops 4294967296 | bytes 12582912 | tf_op jit(solution)/shard_map/prefix_attention/pallas_call | solution.py:164
  (32 shorter events, 0.7 us)
Async XLA Ops:
  0.0 13.6 %copy-start.4 = (s32[2]{0:T(128)S(1)}, s32[2]{0:T(128)}, u32[]{:S(2)}) copy-start(s32[2]{0:T(128)} %count_ref.1) | copy-start | bytes 28
  0.0 13.7 %copy-start.7 = (s32[2,16]{1,0:T(2,128)S(1)}, s32[2,16]{1,0:T(2,128)}, u32[]{:S(2)}) copy-start(s32[2,16]{1,0:T(2,128)} %param.11) | copy-start | bytes 388
  0.0 13.8 %copy-start.6 = (s32[512]{0:T(512)S(1)}, s32[512]{0:T(512)}, u32[]{:S(2)}) copy-start(s32[512]{0:T(512)} %param.13) | copy-start | bytes 6148
  1.9 27.0 %all-to-all-start = ((bf16[8,2,64,256]{3,2,1,0:T(8,128)(2,1)}), bf16[8,2,64,256]{3,2,1,0:T(8,128)(2,1)S(1)}, u32[]{:S(2)}, u32[]{:S(2)}) async-start(bf16[8,2,64,256]{3,2,1,0:T(8,128)(2,1)} %bitcast.14), calls=%async_computation | async-start | bytes 1048576 | tf_op jit(solution)/shard_map/all_to_all | solution.py:222
  14.0 1.9 %collective-permute-start = (s32[1,32]{1,0:T(1,128)S(1)}, s32[1,32]{1,0:T(1,128)S(1)}, u32[]{:S(2)}, u32[]{:S(2)}) collective-permute-start(s32[1,32]{1,0:T(1,128)S(1)} %bitcast_select_fusion), channel_id=1, source_target_pairs={{0,8},{8,0},{16,24},{24,16},{32,40},{40,32},{48,56},{56,48},{64,72... | collective-permute-start | bytes 392 | tf_op jit(solution)/shard_map/ppermute | solution.py:198
  15.9 3.9 %collective-permute-start.3 = (s32[2,32]{1,0:T(2,128)S(1)}, s32[2,32]{1,0:T(2,128)S(1)}, u32[]{:S(2)}, u32[]{:S(2)}) collective-permute-start(s32[2,32]{1,0:T(2,128)S(1)} %pad_add_fusion), channel_id=1, source_target_pairs={{0,48},{8,56},{16,32},{24,40},{32,16},{40,24},{48,0},{56,8},{64,11... | collective-permute-start | bytes 776 | tf_op jit(solution)/shard_map/ppermute | solution.py:198
  18.4 4.2 %collective-permute-start.2 = (s32[2,32]{1,0:T(2,128)S(1)}, s32[2,32]{1,0:T(2,128)S(1)}, u32[]{:S(2)}, u32[]{:S(2)}) collective-permute-start(s32[2,32]{1,0:T(2,128)S(1)} %pad_add_fusion), channel_id=1, source_target_pairs={{0,32},{8,40},{16,48},{24,56},{32,0},{40,8},{48,16},{56,24},{64,96... | collective-permute-start | bytes 776 | tf_op jit(solution)/shard_map/ppermute | solution.py:198
  18.9 3.7 %collective-permute-start.1 = (s32[2,32]{1,0:T(2,128)S(1)}, s32[2,32]{1,0:T(2,128)S(1)}, u32[]{:S(2)}, u32[]{:S(2)}) collective-permute-start(s32[2,32]{1,0:T(2,128)S(1)} %pad_add_fusion), channel_id=1, source_target_pairs={{0,16},{8,24},{16,0},{24,8},{32,48},{40,56},{48,32},{56,40},{64,80... | collective-permute-start | bytes 776 | tf_op jit(solution)/shard_map/ppermute | solution.py:198
  22.6 4.6 %collective-permute-start.6 = (s32[8,32]{1,0:T(8,128)S(1)}, s32[8,32]{1,0:T(8,128)S(1)}, u32[]{:S(2)}, u32[]{:S(2)}) collective-permute-start(s32[8,32]{1,0:T(8,128)S(1)} %concatenate.12), channel_id=1, source_target_pairs={{0,192},{8,200},{16,208},{24,216},{32,224},{40,232},{48,240},{56,2... | collective-permute-start | bytes 3080 | tf_op jit(solution)/shard_map/ppermute | solution.py:198
  24.3 3.7 %collective-permute-start.5 = (s32[8,32]{1,0:T(8,128)S(1)}, s32[8,32]{1,0:T(8,128)S(1)}, u32[]{:S(2)}, u32[]{:S(2)}) collective-permute-start(s32[8,32]{1,0:T(8,128)S(1)} %concatenate.12), channel_id=1, source_target_pairs={{0,128},{8,136},{16,144},{24,152},{32,160},{40,168},{48,176},{56,1... | collective-permute-start | bytes 3080 | tf_op jit(solution)/shard_map/ppermute | solution.py:198
  24.4 3.7 %collective-permute-start.4 = (s32[8,32]{1,0:T(8,128)S(1)}, s32[8,32]{1,0:T(8,128)S(1)}, u32[]{:S(2)}, u32[]{:S(2)}) collective-permute-start(s32[8,32]{1,0:T(8,128)S(1)} %concatenate.12), channel_id=1, source_target_pairs={{0,64},{8,72},{16,80},{24,88},{32,96},{40,104},{48,112},{56,120},{... | collective-permute-start | bytes 3080 | tf_op jit(solution)/shard_map/ppermute | solution.py:198
  28.9 0.8 copy-start.5
  32.8 11.2 %copy-start.2 = (bf16[1024,256]{1,0:T(8,128)(2,1)S(1)}, bf16[1024,256]{1,0:T(8,128)(2,1)}, u32[]{:S(2)}) copy-start(bf16[1024,256]{1,0:T(8,128)(2,1)} %kv_ref.1) | copy-start | bytes 1572868
  32.8 11.2 %copy-start.3 = (s32[2]{0:T(128)S(1)}, s32[2]{0:T(128)}, u32[]{:S(2)}) copy-start(s32[2]{0:T(128)} %owner_ref.3) | copy-start | bytes 28
  32.8 59.0 %all-to-all-start.1 = ((bf16[64,64,256]{2,1,0:T(8,128)(2,1)}), bf16[64,64,256]{2,1,0:T(8,128)(2,1)S(1)}, u32[]{:S(2)}, u32[]{:S(2)}) async-start(bf16[64,64,256]{2,1,0:T(8,128)(2,1)} %pick_blocks.1), calls=%async_computation.1 | async-start | bytes 4194304 | tf_op jit(solution)/shard_map/all_to_all | solution.py:225
  44.0 1.6 %copy-start = (bf16[1024,1024]{1,0:T(8,128)(2,1)S(1)}, bf16[1024,1024]{1,0:T(8,128)(2,1)}, u32[]{:S(2)}) copy-start(bf16[1024,1024]{1,0:T(8,128)(2,1)} %q_ref.3) | copy-start | bytes 6291460
  91.8 1.6 %copy-start.1 = (bf16[1024,1024]{1,0:T(8,128)(2,1)S(1)}, bf16[1024,1024]{1,0:T(8,128)(2,1)}, u32[]{:S(2)}) copy-start(bf16[1024,1024]{1,0:T(8,128)(2,1)} %q_ref.3) | copy-start | bytes 6291460

commit v3 on v2

v3 whole, which is shorter than its diff:
```python
import functools
import math

import jax
import jax.numpy as jnp
from jax import lax
from jax.experimental import pallas as pl
from jax.experimental.pallas import tpu as pltpu
from jax.sharding import PartitionSpec as P

HD = 128
REQ_DEV = 2
PREF = 16
PB = 64
SLOT_CAP = 2
MIN_LIVE = 12
PICK_STEP = 16
ROW_TILE = 256
EXP_SCALE = math.log2(math.e) / math.sqrt(HD)
MASKED = -1e30
HEAD_STEP = 2
KEY_BOUND = 6.0
EXP2_LIMIT = 112.0
FRESH_VMEM_LIMIT = 51712 * 1024
PREFIX_VMEM_LIMIT = 51712 * 1024
PICK_VMEM_LIMIT = 8 * 1024 * 1024


def pick_blocks(wanted, me, group_store):
    groups = wanted.shape[0] // SLOT_CAP
    block_shape = group_store.shape[1:]

    def kernel(wanted_ref, me_ref, store_ref, out_ref):
        first = pl.program_id(0) * PICK_STEP
        for i in range(PICK_STEP):
            for j in range(SLOT_CAP):
                at = ((first + i) ^ me_ref[0]) * SLOT_CAP + j
                out_ref[SLOT_CAP * i + j] = store_ref[wanted_ref[at]]

    return pl.pallas_call(
        kernel,
        grid_spec=pltpu.PrefetchScalarGridSpec(
            num_scalar_prefetch=2,
            grid=(groups // PICK_STEP,),
            in_specs=[pl.BlockSpec(memory_space=pltpu.VMEM)],
            out_specs=pl.BlockSpec((SLOT_CAP * PICK_STEP,) + block_shape, lambda i, *_: (i, 0, 0)),
        ),
        out_shape=jax.ShapeDtypeStruct((SLOT_CAP * groups,) + block_shape, group_store.dtype),
        compiler_params=pltpu.CompilerParams(vmem_limit_bytes=PICK_VMEM_LIMIT),
        name="pick_blocks",
    )(wanted, me, group_store)


def scores_of(query_tile, keys):
    return lax.dot_general(
        query_tile, keys, (((1,), (1,)), ((), ())), preferred_element_type=jnp.float32
    )


def fresh_attention(queries, new_kv, slot_request):
    rows, width = queries.shape
    steps = width // HD // HEAD_STEP
    span = rows // slot_request.shape[0]

    def kernel(owner_ref, q_ref, kv_ref, acc_ref, stat_ref, excess_ref, v_ext):
        @pl.when(pl.program_id(0) == 0)
        def _():
            v_ext[:, :HD] = kv_ref[:, HD:]
            v_ext[:, HD:] = jnp.ones((rows, HD), v_ext.dtype)

        same = owner_ref[0] == owner_ref[1]
        lane = lax.broadcasted_iota(jnp.int32, (ROW_TILE, HD), 1)
        excess = None
        for first in range(0, rows, ROW_TILE):
            last = first + ROW_TILE
            stat = jnp.zeros((ROW_TILE, HD), jnp.float32)
            for part in range(HEAD_STEP):
                column = slice(part * HD, (part + 1) * HD)
                q = q_ref[first:last, column]
                s = scores_of(q, kv_ref[:last, :HD])
                key = lax.broadcasted_iota(jnp.int32, s.shape, 1)
                row = first + lax.broadcasted_iota(jnp.int32, s.shape, 0)
                own = (first // span) * span
                lowest = jnp.where(same, 0, own)
                s = jnp.where((key <= row) & (key >= lowest), s, MASKED)
                top = jnp.max(s, axis=1, keepdims=True)
                p = jnp.exp2((s - top) * EXP_SCALE).astype(jnp.bfloat16)
                o = jnp.dot(p, v_ext[:last, :], preferred_element_type=jnp.float32)
                acc_ref[first:last, column] = o[:, :HD]
                stat = jnp.where(lane == 2 * part, top, jnp.where(lane == 2 * part + 1, o[:, HD:], stat))
                reach = KEY_BOUND * jnp.sum(jnp.abs(q.astype(jnp.float32)), axis=1, keepdims=True)
                over = jnp.max((reach - top) * EXP_SCALE)
                excess = over if excess is None else jnp.maximum(excess, over)
            stat_ref[0, first:last, :] = stat
        excess_ref[pl.program_id(0)] = excess

    return pl.pallas_call(
        kernel,
        grid_spec=pltpu.PrefetchScalarGridSpec(
            num_scalar_prefetch=1,
            grid=(steps,),
            in_specs=[
                pl.BlockSpec((rows, HEAD_STEP * HD), lambda h, owner: (0, h)),
                pl.BlockSpec((rows, 2 * HD), lambda h, owner: (0, 0)),
            ],
            out_specs=[
                pl.BlockSpec((rows, HEAD_STEP * HD), lambda h, owner: (0, h)),
                pl.BlockSpec((1, rows, HD), lambda h, owner: (h, 0, 0)),
                pl.BlockSpec(memory_space=pltpu.SMEM),
            ],
            scratch_shapes=[pltpu.VMEM((rows, 2 * HD), jnp.bfloat16)],
        ),
        out_shape=[
            jax.ShapeDtypeStruct((rows, width), jnp.float32),
            jax.ShapeDtypeStruct((steps, rows, HD), jnp.float32),
            jax.ShapeDtypeStruct((steps,), jnp.float32),
        ],
        compiler_params=pltpu.CompilerParams(vmem_limit_bytes=FRESH_VMEM_LIMIT),
        cost_estimate=pl.CostEstimate(
            flops=4 * rows * rows * width, bytes_accessed=12 * rows * width, transcendentals=rows * rows * width // HD
        ),
        name="fresh_attention",
    )(slot_request, queries, new_kv)


def prefix_attention(queries, received, acc, stat, excess, slot_request, places, prefix_count):
    rows, width = queries.shape
    steps = width // HD // HEAD_STEP
    step_width = HEAD_STEP * HD
    slots = slot_request.shape[0]
    span = rows // slots
    keys = PREF * PB
    sure = MIN_LIVE * PB

    def kernel(
        owner_ref, place_ref, count_ref, excess_ref, q_any, recv_ref, acc_any, stat_any, out_any,
        k_scr, v_scr, q_scr, acc_scr, stat_scr, out_scr, in_sem, out_sem,
    ):
        def gather(i, carry):
            request, to = i // PREF, pl.ds(pl.multiple_of((i % PREF) * PB, PB), PB)
            block = recv_ref[place_ref[i]]
            k_scr[request, to, :] = block[:, :HD]
            v_scr[request, to, :HD] = block[:, HD:]
            return carry

        def in_copies(step):
            column = pl.ds(pl.multiple_of(step * step_width, step_width), step_width)
            return (
                pltpu.make_async_copy(q_any.at[:, column], q_scr.at[step], in_sem.at[step, 0]),
                pltpu.make_async_copy(acc_any.at[:, column], acc_scr.at[step], in_sem.at[step, 1]),
                pltpu.make_async_copy(stat_any.at[step], stat_scr.at[step], in_sem.at[step, 2]),
            )

        def out_copy(step):
            column = pl.ds(pl.multiple_of(step * step_width, step_width), step_width)
            return pltpu.make_async_copy(out_scr.at[step], out_any.at[:, column], out_sem.at[step])

        for copy in in_copies(0):
            copy.start()
        v_scr[:, :, HD:] = jnp.ones((REQ_DEV, keys, HD), v_scr.dtype)
        lax.fori_loop(0, REQ_DEV * PREF, gather, 0, unroll=4)

        def attend(step, with_maximum):
            for part in range(HEAD_STEP):
                column = slice(part * HD, (part + 1) * HD)
                for slot in range(slots):
                    owner = owner_ref[slot]
                    live = count_ref[owner] * PB
                    for first in range(slot * span, (slot + 1) * span, ROW_TILE):
                        tile = slice(first, first + ROW_TILE)
                        s = scores_of(q_scr[step, tile, column], k_scr[owner])
                        key = sure + lax.broadcasted_iota(jnp.int32, (ROW_TILE, keys - sure), 1)
                        s = jnp.concatenate([s[:, :sure], jnp.where(key < live, s[:, sure:], MASKED)], axis=1)
                        top = stat_scr[step, tile, 2 * part : 2 * part + 1]
                        total = stat_scr[step, tile, 2 * part + 1 : 2 * part + 2]
                        total_acc = acc_scr[step, tile, column]
                        if with_maximum:
                            old_top = top
                            top = jnp.maximum(old_top, jnp.max(s, axis=1, keepdims=True))
                            keep = jnp.exp2((old_top - top) * EXP_SCALE)
                            total, total_acc = total * keep, total_acc * keep
                        p = jnp.exp2((s - top) * EXP_SCALE).astype(jnp.bfloat16)
                        o = jnp.dot(p, v_scr[owner], preferred_element_type=jnp.float32)
                        result = (total_acc + o[:, :HD]) / (total + o[:, HD:])
                        out_scr[step, tile, column] = result.astype(out_scr.dtype)

        def one_step(step, carry):
            @pl.when(step + 1 < steps)
            def _():
                for copy in in_copies(step + 1):
                    copy.start()

            for copy in in_copies(step):
                copy.wait()
            bounded = excess_ref[step] < EXP2_LIMIT

            @pl.when(bounded)
            def _():
                attend(step, False)

            @pl.when(jnp.logical_not(bounded))
            def _():
                attend(step, True)

            out_copy(step).start()
            return carry

        lax.fori_loop(0, steps, one_step, 0)
        for step in range(steps):
            out_copy(step).wait()

    smem, anywhere = pl.BlockSpec(memory_space=pltpu.SMEM), pl.BlockSpec(memory_space=pl.ANY)
    return pl.pallas_call(
        kernel,
        in_specs=[smem] * 4 + [anywhere, pl.BlockSpec(memory_space=pltpu.VMEM), anywhere, anywhere],
        out_specs=anywhere,
        scratch_shapes=[
            pltpu.VMEM((REQ_DEV, keys, HD), jnp.bfloat16),
            pltpu.VMEM((REQ_DEV, keys, 2 * HD), jnp.bfloat16),
            pltpu.VMEM((steps, rows, step_width), jnp.bfloat16),
            pltpu.VMEM((steps, rows, step_width), jnp.float32),
            pltpu.VMEM((steps, rows, HD), jnp.float32),
            pltpu.VMEM((steps, rows, step_width), jnp.bfloat16),
            pltpu.SemaphoreType.DMA((steps, 3)),
            pltpu.SemaphoreType.DMA((steps,)),
        ],
        out_shape=jax.ShapeDtypeStruct((rows, width), jnp.bfloat16),
        compiler_params=pltpu.CompilerParams(vmem_limit_bytes=PREFIX_VMEM_LIMIT),
        cost_estimate=pl.CostEstimate(
            flops=4 * rows * keys * width, bytes_accessed=12 * rows * width, transcendentals=rows * keys * width // HD
        ),
        name="prefix_attention",
    )(slot_request, places, prefix_count, excess, queries, received, acc, stat)


def used_rows(prefix_ids, prefix_count, block_row):
    known = jnp.arange(block_row.shape[0], dtype=jnp.int32)
    ids = prefix_ids.reshape(-1)
    rows = jnp.sum(jnp.where(ids[:, None] == known, block_row, 0), axis=-1)
    live = (jnp.arange(PREF, dtype=jnp.int32)[None, :] < prefix_count[:, None]).reshape(-1)
    return jnp.where(live, rows, -1)


def share_over_req(values):
    groups = lax.axis_size("req")
    known = values[None, :]
    for steps in ((1,), (2, 4, 6), (8, 16, 24)):
        parts = [lax.ppermute(known, "req", [(d, d ^ step) for d in range(groups)]) for step in steps]
        known = jnp.concatenate([known] + parts, axis=0)
    return known


def low_high(rows, first_row, group_rows):
    within = rows - first_row
    member = (within >= 0) & (within < group_rows)
    low = jnp.min(jnp.where(member, within, group_rows), axis=-1)
    high = jnp.max(jnp.where(member, within, 0), axis=-1)
    return jnp.minimum(low, high), high


def on_device(queries, new_kv, pool_kv, slot_request, prefix_ids, prefix_count, block_row):
    tp_count = lax.axis_size("tp")
    groups = lax.axis_size("req")
    me = lax.axis_index("req").astype(jnp.int32)
    pool_local = pool_kv.shape[0]
    head_width = pool_kv.shape[2] // tp_count
    group_rows = tp_count * pool_local
    rows = used_rows(prefix_ids, prefix_count, block_row)
    low, high = low_high(share_over_req(rows), me * group_rows, group_rows)
    wanted = jnp.stack([low, high], axis=1).reshape(-1)
    by_head = pool_kv.reshape(pool_local, PB, tp_count, head_width).transpose(2, 0, 1, 3)
    group_store = lax.all_to_all(by_head, "tp", split_axis=0, concat_axis=0, tiled=True)
    group_store = group_store.reshape(group_rows, PB, head_width)
    to_send = pick_blocks(wanted, me[None], group_store)
    received = lax.all_to_all(to_send, "req", split_axis=0, concat_axis=0, tiled=True)
    same_group = rows[:, None] // group_rows == rows[None, :] // group_rows
    is_high = jnp.any(same_group & (rows[None, :] < rows[:, None]) & (rows[None, :] >= 0), axis=1)
    places = jnp.where(rows >= 0, SLOT_CAP * (rows // group_rows) + is_high.astype(jnp.int32), 0)
    acc, stat, excess = fresh_attention(queries, new_kv, slot_request)
    return prefix_attention(queries, received, acc, stat, excess, slot_request, places, prefix_count)


def solution(mesh):
    return jax.shard_map(
        on_device,
        mesh=mesh,
        in_specs=(
            P("req", "tp"),
            P("req", "tp"),
            P(("req", "tp"), None, None),
            P("req"),
            P("req", None),
            P("req"),
            P(),
        ),
        out_specs=P("req", "tp"),
        check_vma=False,
    )
```

time: 114 us -> 108 us (0.947)
  Pallas kernels: 40.1 us -> 33.2 us
  waiting for transfers between devices: 35.6 us -> 38.8 us
  local copies, waits for them, and re-layouts: 6.95 us -> 3.79 us
    all_to_all x1, waiting for transfers between devices: 29.6 us -> 32.7 us  [on_device(): lax.all_to_all(to_send, 'req', split_axis=0, concat_axis=0, tiled=True)]
    pallas_call x1, Pallas kernels: 16.7 us -> 13.8 us  [fresh_attention(): pl.pallas_call(kernel, grid_spec=pltpu.PrefetchScalarGridSpec(num_scalar_...]
    pallas_call x1, Pallas kernels: 20.4 us -> 17.5 us  [prefix_attention(): pl.pallas_call(kernel, in_specs=[smem] * 4 + [anywhere, pl.BlockSpec(memo...]
    unnamed x16 -> x14, local copies, waits for them, and re-layouts: 3.99 us -> 1.37 us
    pallas_call x1, Pallas kernels: 3.11 us -> 1.96 us  [pick_blocks(): pl.pallas_call(kernel, grid_spec=pltpu.PrefetchScalarGridSpec(num_scalar_...]
  transfers between devices with their start and end apart: 9 -> 9, of which waited for: 6 -> 6; matrix products, arithmetic and copies ran while one was open for 1% -> 1% of each run, Pallas kernels for 15% -> 13%
where the time goes in v3:
time: 108 us
  waiting for transfers between devices  38.8 us (36%)
  Pallas kernels  33.2 us (31%)
  starting transfers between devices  31 us (29%)
  local copies, waits for them, and re-layouts  3.79 us (4%)
    all_to_all x1, waiting for transfers between devices, on_device(): lax.all_to_all(to_send, 'req', split_axis=0, concat_axis=0, tiled=True)  32.7 us
    pallas_call x1, Pallas kernels, prefix_attention(): pl.pallas_call(kernel, in_specs=[smem] * 4 + [anywhere, pl.BlockSpec(memo...  17.5 us
    pallas_call x1, Pallas kernels, fresh_attention(): pl.pallas_call(kernel, grid_spec=pltpu.PrefetchScalarGridSpec(num_scalar_...  13.8 us
    all_to_all x1, starting transfers between devices, on_device(): lax.all_to_all(by_head, 'tp', split_axis=0, concat_axis=0, tiled=True)  11.6 us
    all_to_all x1, starting transfers between devices, on_device(): lax.all_to_all(to_send, 'req', split_axis=0, concat_axis=0, tiled=True)  11.5 us
    ppermute x7, starting transfers between devices, share_over_req(): lax.ppermute(known, 'req', [(d, d ^ step) for d in range(groups)])  7.92 us
    ppermute x7, waiting for transfers between devices, share_over_req(): lax.ppermute(known, 'req', [(d, d ^ step) for d in range(groups)])  6.01 us
  transfers between devices with their start and end apart: 9, of which 6 were waited for; matrix products, arithmetic and copies ran while one was open for 1% of the time, Pallas kernels for 13%

profile of v3, /device:TPU:1, one launch (start us, length us, event | category | flops | bytes accessed | tf_op | source)
XLA Modules:
  0.0 107.6 jit_solution(8954850975451017762)
XLA Ops:
  0.0 1.9 %copy.16 = bf16[2,8,8,8,256]{4,3,1,0,2:T(8,128)(2,1)} copy(bf16[2,8,8,8,256]{4,3,2,1,0:T(8,128)(2,1)} %bitcast.16) | data formatting | bytes 1048576 | tf_op jit(solution)/shard_map/reshape | solution.py:271
  1.9 11.6 %all-to-all-start = ((bf16[8,2,64,256]{3,2,1,0:T(8,128)(2,1)}), bf16[8,2,64,256]{3,2,1,0:T(8,128)(2,1)S(1)}, u32[]{:S(2)}, u32[]{:S(2)}) async-start(bf16[8,2,64,256]{3,2,1,0:T(8,128)(2,1)} %bitcast.14), calls=%async_computation | async-start | bytes 1048576 | tf_op jit(solution)/shard_map/all_to_all | solution.py:272
  13.8 0.2 select_reduce_fusion
  14.0 1.0 collective-permute-start
  15.1 0.8 collective-permute-done
  15.9 2.5 %collective-permute-start.3 = (s32[2,32]{1,0:T(2,128)S(1)}, s32[2,32]{1,0:T(2,128)S(1)}, u32[]{:S(2)}, u32[]{:S(2)}) collective-permute-start(s32[2,32]{1,0:T(2,128)S(1)} %pad_add_fusion), channel_id=1, source_target_pairs={{0,48},{8,56},{16,32},{24,40},{32,16},{40,24},{48,0},{56,8},{64,11... | collective-permute-start | bytes 776 | tf_op jit(solution)/shard_map/ppermute | solution.py:248
  18.4 0.5 collective-permute-start.2
  18.9 0.3 collective-permute-start.1
  19.2 0.7 collective-permute-done.3
  19.8 2.8 %collective-permute-done.2 = s32[2,32]{1,0:T(2,128)S(1)} collective-permute-done((s32[2,32]{1,0:T(2,128)S(1)}, s32[2,32]{1,0:T(2,128)S(1)}, u32[]{:S(2)}, u32[]{:S(2)}) %collective-permute-start.2) | collective-permute-done | bytes 288 | tf_op jit(solution)/shard_map/ppermute | solution.py:248
  22.6 1.7 %collective-permute-start.6 = (s32[8,32]{1,0:T(8,128)S(1)}, s32[8,32]{1,0:T(8,128)S(1)}, u32[]{:S(2)}, u32[]{:S(2)}) collective-permute-start(s32[8,32]{1,0:T(8,128)S(1)} %concatenate.12), channel_id=1, source_target_pairs={{0,192},{8,200},{16,208},{24,216},{32,224},{40,232},{48,240},{56,2... | collective-permute-start | bytes 3080 | tf_op jit(solution)/shard_map/ppermute | solution.py:248
  24.4 1.9 %collective-permute-start.4 = (s32[8,32]{1,0:T(8,128)S(1)}, s32[8,32]{1,0:T(8,128)S(1)}, u32[]{:S(2)}, u32[]{:S(2)}) collective-permute-start(s32[8,32]{1,0:T(8,128)S(1)} %concatenate.12), channel_id=1, source_target_pairs={{0,64},{8,72},{16,80},{24,88},{32,96},{40,104},{48,112},{56,120},{... | collective-permute-start | bytes 3080 | tf_op jit(solution)/shard_map/ppermute | solution.py:248
  26.3 1.0 collective-permute-done.6
  27.3 0.7 collective-permute-done.5
  28.0 0.1 select_reduce_fusion.2
  28.2 0.1 copy.12
  28.3 0.1 reshape.157.wanted_ref
  28.4 2.0 %pick_blocks.1 = bf16[64,64,256]{2,1,0:T(8,128)(2,1)} custom-call(s32[64]{0:T(128)S(1)} %reshape.157.wanted_ref, s32[1]{0:T(128)} %bitcast.3.me_ref, bf16[16,64,256]{2,1,0:T(8,128)(2,1)S(1)} %bitcast.15), custom_call_target="tpu_custom_call" | custom-call | tf_op jit(solution)/shard_map/pick_blocks/pallas_call | solution.py:40
  30.3 11.5 %all-to-all-start.1 = ((bf16[64,64,256]{2,1,0:T(8,128)(2,1)}), bf16[64,64,256]{2,1,0:T(8,128)(2,1)}, u32[]{:S(2)}, u32[]{:S(2)}) async-start(bf16[64,64,256]{2,1,0:T(8,128)(2,1)} %pick_blocks.1), calls=%async_computation.1 | async-start | bytes 4194304 | tf_op jit(solution)/shard_map/all_to_all | solution.py:275
  41.9 0.2 and_reduce_fusion
  42.1 13.8 %fresh_attention.1 = (f32[1024,1024]{1,0:T(8,128)}, f32[4,1024,128]{2,1,0:T(8,128)S(1)}, f32[4]{0:T(128)S(1)}) custom-call(s32[2]{0:T(128)S(1)} %copy-done.2, bf16[1024,1024]{1,0:T(8,128)(2,1)} %q_any.1, bf16[1024,256]{1,0:T(8,128)(2,1)S(1)} %copy-done.1), custom_call_target="tpu_custom_call" | custom-call | flops 4294967296 | bytes 12582912 | tf_op jit(solution)/shard_map/fresh_attention/pallas_call | solution.py:97
  55.9 1.3 %copy-done.4 = f32[4,1024,128]{2,1,0:T(8,128)} copy-done((f32[4,1024,128]{2,1,0:T(8,128)}, f32[4,1024,128]{2,1,0:T(8,128)S(1)}, u32[]{:S(2)}) %copy-start.4) | copy-done | bytes 2097176
  57.2 32.7 %all-to-all-done.1.recv_ref = bf16[64,64,256]{2,1,0:T(8,128)(2,1)} async-done(((bf16[64,64,256]{2,1,0:T(8,128)(2,1)}), bf16[64,64,256]{2,1,0:T(8,128)(2,1)}, u32[]{:S(2)}, u32[]{:S(2)}) %all-to-all-start.1) | async-done | bytes 2097184 | tf_op jit(solution)/shard_map/all_to_all | solution.py:275
  90.0 17.5 %prefix_attention.1 = bf16[1024,1024]{1,0:T(8,128)(2,1)} custom-call(s32[2]{0:T(128)S(1)} %copy-done.2, s32[32]{0:T(128)S(1)} %add_select_fusion.place_ref, s32[2]{0:T(128)S(1)} %copy-done.3, f32[4]{0:T(128)S(1)} %get-tuple-element.8.excess_ref, bf16[1024,1024]{1,0:T(8,128)(2,1)S(1)} %copy-done, bf16[64,64,256]{2,1,0:T(8,128)(2,1)} %all-to-all-done.1.recv_ref, ...), custom_call_target="tpu_custom_call" | custom-call | flops 4294967296 | bytes 12582912 | tf_op jit(solution)/shard_map/prefix_attention/pallas_call | solution.py:213
  (30 shorter events, 0.5 us)
Async XLA Ops:
  0.0 13.6 %copy-start.3 = (s32[2]{0:T(128)S(1)}, s32[2]{0:T(128)}, u32[]{:S(2)}) copy-start(s32[2]{0:T(128)} %count_ref.1) | copy-start | bytes 28
  0.0 13.7 %copy-start.6 = (s32[2,16]{1,0:T(2,128)S(1)}, s32[2,16]{1,0:T(2,128)}, u32[]{:S(2)}) copy-start(s32[2,16]{1,0:T(2,128)} %param.11) | copy-start | bytes 388
  0.0 13.8 %copy-start.5 = (s32[512]{0:T(512)S(1)}, s32[512]{0:T(512)}, u32[]{:S(2)}) copy-start(s32[512]{0:T(512)} %param.13) | copy-start | bytes 6148
  1.9 26.4 %all-to-all-start = ((bf16[8,2,64,256]{3,2,1,0:T(8,128)(2,1)}), bf16[8,2,64,256]{3,2,1,0:T(8,128)(2,1)S(1)}, u32[]{:S(2)}, u32[]{:S(2)}) async-start(bf16[8,2,64,256]{3,2,1,0:T(8,128)(2,1)} %bitcast.14), calls=%async_computation | async-start | bytes 1048576 | tf_op jit(solution)/shard_map/all_to_all | solution.py:272
  14.0 1.9 %collective-permute-start = (s32[1,32]{1,0:T(1,128)S(1)}, s32[1,32]{1,0:T(1,128)S(1)}, u32[]{:S(2)}, u32[]{:S(2)}) collective-permute-start(s32[1,32]{1,0:T(1,128)S(1)} %bitcast_select_fusion), channel_id=1, source_target_pairs={{0,8},{8,0},{16,24},{24,16},{32,40},{40,32},{48,56},{56,48},{64,72... | collective-permute-start | bytes 392 | tf_op jit(solution)/shard_map/ppermute | solution.py:248
  15.9 3.9 %collective-permute-start.3 = (s32[2,32]{1,0:T(2,128)S(1)}, s32[2,32]{1,0:T(2,128)S(1)}, u32[]{:S(2)}, u32[]{:S(2)}) collective-permute-start(s32[2,32]{1,0:T(2,128)S(1)} %pad_add_fusion), channel_id=1, source_target_pairs={{0,48},{8,56},{16,32},{24,40},{32,16},{40,24},{48,0},{56,8},{64,11... | collective-permute-start | bytes 776 | tf_op jit(solution)/shard_map/ppermute | solution.py:248
  18.4 4.2 %collective-permute-start.2 = (s32[2,32]{1,0:T(2,128)S(1)}, s32[2,32]{1,0:T(2,128)S(1)}, u32[]{:S(2)}, u32[]{:S(2)}) collective-permute-start(s32[2,32]{1,0:T(2,128)S(1)} %pad_add_fusion), channel_id=1, source_target_pairs={{0,32},{8,40},{16,48},{24,56},{32,0},{40,8},{48,16},{56,24},{64,96... | collective-permute-start | bytes 776 | tf_op jit(solution)/shard_map/ppermute | solution.py:248
  18.9 3.7 %collective-permute-start.1 = (s32[2,32]{1,0:T(2,128)S(1)}, s32[2,32]{1,0:T(2,128)S(1)}, u32[]{:S(2)}, u32[]{:S(2)}) collective-permute-start(s32[2,32]{1,0:T(2,128)S(1)} %pad_add_fusion), channel_id=1, source_target_pairs={{0,16},{8,24},{16,0},{24,8},{32,48},{40,56},{48,32},{56,40},{64,80... | collective-permute-start | bytes 776 | tf_op jit(solution)/shard_map/ppermute | solution.py:248
  22.6 4.6 %collective-permute-start.6 = (s32[8,32]{1,0:T(8,128)S(1)}, s32[8,32]{1,0:T(8,128)S(1)}, u32[]{:S(2)}, u32[]{:S(2)}) collective-permute-start(s32[8,32]{1,0:T(8,128)S(1)} %concatenate.12), channel_id=1, source_target_pairs={{0,192},{8,200},{16,208},{24,216},{32,224},{40,232},{48,240},{56,2... | collective-permute-start | bytes 3080 | tf_op jit(solution)/shard_map/ppermute | solution.py:248
  24.3 3.7 %collective-permute-start.5 = (s32[8,32]{1,0:T(8,128)S(1)}, s32[8,32]{1,0:T(8,128)S(1)}, u32[]{:S(2)}, u32[]{:S(2)}) collective-permute-start(s32[8,32]{1,0:T(8,128)S(1)} %concatenate.12), channel_id=1, source_target_pairs={{0,128},{8,136},{16,144},{24,152},{32,160},{40,168},{48,176},{56,1... | collective-permute-start | bytes 3080 | tf_op jit(solution)/shard_map/ppermute | solution.py:248
  24.4 3.7 %collective-permute-start.4 = (s32[8,32]{1,0:T(8,128)S(1)}, s32[8,32]{1,0:T(8,128)S(1)}, u32[]{:S(2)}, u32[]{:S(2)}) collective-permute-start(s32[8,32]{1,0:T(8,128)S(1)} %concatenate.12), channel_id=1, source_target_pairs={{0,64},{8,72},{16,80},{24,88},{32,96},{40,104},{48,112},{56,120},{... | collective-permute-start | bytes 3080 | tf_op jit(solution)/shard_map/ppermute | solution.py:248
  30.3 11.8 %copy-start.1 = (bf16[1024,256]{1,0:T(8,128)(2,1)S(1)}, bf16[1024,256]{1,0:T(8,128)(2,1)}, u32[]{:S(2)}) copy-start(bf16[1024,256]{1,0:T(8,128)(2,1)} %kv_ref.1) | copy-start | bytes 1572868
  30.3 11.8 %copy-start.2 = (s32[2]{0:T(128)S(1)}, s32[2]{0:T(128)}, u32[]{:S(2)}) copy-start(s32[2]{0:T(128)} %owner_ref.3) | copy-start | bytes 28
  30.3 59.6 %all-to-all-start.1 = ((bf16[64,64,256]{2,1,0:T(8,128)(2,1)}), bf16[64,64,256]{2,1,0:T(8,128)(2,1)}, u32[]{:S(2)}, u32[]{:S(2)}) async-start(bf16[64,64,256]{2,1,0:T(8,128)(2,1)} %pick_blocks.1), calls=%async_computation.1 | async-start | bytes 4194304 | tf_op jit(solution)/shard_map/all_to_all | solution.py:275
  42.1 47.9 %copy-start = (bf16[1024,1024]{1,0:T(8,128)(2,1)S(1)}, bf16[1024,1024]{1,0:T(8,128)(2,1)}, u32[]{:S(2)}) copy-start(bf16[1024,1024]{1,0:T(8,128)(2,1)} %q_any.1) | copy-start | bytes 6291460
  55.9 1.3 %copy-start.4 = (f32[4,1024,128]{2,1,0:T(8,128)}, f32[4,1024,128]{2,1,0:T(8,128)S(1)}, u32[]{:S(2)}) copy-start(f32[4,1024,128]{2,1,0:T(8,128)S(1)} %get-tuple-element.10.stat_any) | copy-start | bytes 6291460

commit v4 on v3

--- a/solution.py
+++ b/solution.py
@@ -14,7 +14,7 @@
 PB = 64
 SLOT_CAP = 2
 MIN_LIVE = 12
-PICK_STEP = 16
+PICK_STEP = 4
 ROW_TILE = 256
 EXP_SCALE = math.log2(math.e) / math.sqrt(HD)
 MASKED = -1e30
@@ -27,25 +27,34 @@
 
 
 def pick_blocks(wanted, me, group_store):
-    groups = wanted.shape[0] // SLOT_CAP
+    count = wanted.shape[0]
     block_shape = group_store.shape[1:]
-
-    def kernel(wanted_ref, me_ref, store_ref, out_ref):
-        first = pl.program_id(0) * PICK_STEP
-        for i in range(PICK_STEP):
-            for j in range(SLOT_CAP):
-                at = ((first + i) ^ me_ref[0]) * SLOT_CAP + j
-                out_ref[SLOT_CAP * i + j] = store_ref[wanted_ref[at]]
-
+    step_blocks = SLOT_CAP * PICK_STEP
+    steps = count // step_blocks
+
+    def kernel(wanted_ref, me_ref, store_ref, out_any, picked, sems):
+        def send(step):
+            blocks = pl.ds(step * step_blocks, step_blocks)
+            return pltpu.make_async_copy(picked.at[blocks], out_any.at[blocks], sems.at[step])
+
+        for step in range(steps):
+            for i in range(step * PICK_STEP, (step + 1) * PICK_STEP):
+                for j in range(SLOT_CAP):
+                    picked[SLOT_CAP * i + j] = store_ref[wanted_ref[(i ^ me_ref[0]) * SLOT_CAP + j]]
+            send(step).start()
+        for step in range(steps):
+            send(step).wait()
+
+    smem = pl.BlockSpec(memory_space=pltpu.SMEM)
     return pl.pallas_call(
         kernel,
-        grid_spec=pltpu.PrefetchScalarGridSpec(
-            num_scalar_prefetch=2,
-            grid=(groups // PICK_STEP,),
-            in_specs=[pl.BlockSpec(memory_space=pltpu.VMEM)],
-            out_specs=pl.BlockSpec((SLOT_CAP * PICK_STEP,) + block_shape, lambda i, *_: (i, 0, 0)),
-        ),
-        out_shape=jax.ShapeDtypeStruct((SLOT_CAP * groups,) + block_shape, group_store.dtype),
+        in_specs=[smem, smem, pl.BlockSpec(memory_space=pltpu.VMEM)],
+        out_specs=pl.BlockSpec(memory_space=pl.ANY),
+        scratch_shapes=[
+            pltpu.VMEM((count,) + block_shape, group_store.dtype),
+            pltpu.SemaphoreType.DMA((steps,)),
+        ],
+        out_shape=jax.ShapeDtypeStruct((count,) + block_shape, group_store.dtype),
         compiler_params=pltpu.CompilerParams(vmem_limit_bytes=PICK_VMEM_LIMIT),
         name="pick_blocks",
     )(wanted, me, group_store)
@@ -133,14 +142,19 @@
     sure = MIN_LIVE * PB
 
     def kernel(
-        owner_ref, place_ref, count_ref, excess_ref, q_any, recv_ref, acc_any, stat_any, out_any,
-        k_scr, v_scr, q_scr, acc_scr, stat_scr, out_scr, in_sem, out_sem,
+        owner_ref, place_ref, count_ref, excess_ref, q_any, recv_any, acc_any, stat_any, out_any,
+        kv_scr, v_scr, q_scr, acc_scr, stat_scr, out_scr, kv_sem, in_sem, out_sem,
     ):
-        def gather(i, carry):
+        def kv_copy(i):
             request, to = i // PREF, pl.ds(pl.multiple_of((i % PREF) * PB, PB), PB)
-            block = recv_ref[place_ref[i]]
-            k_scr[request, to, :] = block[:, :HD]
-            v_scr[request, to, :HD] = block[:, HD:]
+            return pltpu.make_async_copy(recv_any.at[place_ref[i]], kv_scr.at[request, to, :], kv_sem.at[i])
+
+        def start_kv(i, carry):
+            kv_copy(i).start()
+            return carry
+
+        def wait_kv(i, carry):
+            kv_copy(i).wait()
             return carry
 
         def in_copies(step):
@@ -155,10 +169,12 @@
             column = pl.ds(pl.multiple_of(step * step_width, step_width), step_width)
             return pltpu.make_async_copy(out_scr.at[step], out_any.at[:, column], out_sem.at[step])
 
+        lax.fori_loop(0, REQ_DEV * PREF, start_kv, 0, unroll=8)
         for copy in in_copies(0):
             copy.start()
         v_scr[:, :, HD:] = jnp.ones((REQ_DEV, keys, HD), v_scr.dtype)
-        lax.fori_loop(0, REQ_DEV * PREF, gather, 0, unroll=4)
+        lax.fori_loop(0, REQ_DEV * PREF, wait_kv, 0, unroll=8)
+        v_scr[:, :, :HD] = kv_scr[:, :, HD:]
 
         def attend(step, with_maximum):
             for part in range(HEAD_STEP):
@@ -168,7 +184,7 @@
                     live = count_ref[owner] * PB
                     for first in range(slot * span, (slot + 1) * span, ROW_TILE):
                         tile = slice(first, first + ROW_TILE)
-                        s = scores_of(q_scr[step, tile, column], k_scr[owner])
+                        s = scores_of(q_scr[step, tile, column], kv_scr[owner, :, :HD])
                         key = sure + lax.broadcasted_iota(jnp.int32, (ROW_TILE, keys - sure), 1)
                         s = jnp.concatenate([s[:, :sure], jnp.where(key < live, s[:, sure:], MASKED)], axis=1)
                         top = stat_scr[step, tile, 2 * part : 2 * part + 1]
@@ -212,15 +228,16 @@
     smem, anywhere = pl.BlockSpec(memory_space=pltpu.SMEM), pl.BlockSpec(memory_space=pl.ANY)
     return pl.pallas_call(
         kernel,
-        in_specs=[smem] * 4 + [anywhere, pl.BlockSpec(memory_space=pltpu.VMEM), anywhere, anywhere],
+        in_specs=[smem] * 4 + [anywhere] * 4,
         out_specs=anywhere,
         scratch_shapes=[
-            pltpu.VMEM((REQ_DEV, keys, HD), jnp.bfloat16),
+            pltpu.VMEM((REQ_DEV, keys, 2 * HD), jnp.bfloat16),
             pltpu.VMEM((REQ_DEV, keys, 2 * HD), jnp.bfloat16),
             pltpu.VMEM((steps, rows, step_width), jnp.bfloat16),
             pltpu.VMEM((steps, rows, step_width), jnp.float32),
             pltpu.VMEM((steps, rows, HD), jnp.float32),
             pltpu.VMEM((steps, rows, step_width), jnp.bfloat16),
+            pltpu.SemaphoreType.DMA((REQ_DEV * PREF,)),
             pltpu.SemaphoreType.DMA((steps, 3)),
             pltpu.SemaphoreType.DMA((steps,)),
         ],

time: 108 us -> 108 us (level)
  no operation moved by 1% of the time
where the time goes in v4:
time: 108 us; the launch traced here: 107 us
  waiting for transfers between devices  38.8 us (36%)
  Pallas kernels  32.9 us (30%)
  starting transfers between devices  31 us (29%)
  local copies, waits for them, and re-layouts  3.79 us (4%)
    all_to_all x1, waiting for transfers between devices, on_device(): lax.all_to_all(to_send, 'req', split_axis=0, concat_axis=0, tiled=True)  32.7 us
    pallas_call x1, Pallas kernels, prefix_attention(): pl.pallas_call(kernel, in_specs=[smem] * 4 + [anywhere] * 4, out_specs=an...  17.2 us
    pallas_call x1, Pallas kernels, fresh_attention(): pl.pallas_call(kernel, grid_spec=pltpu.PrefetchScalarGridSpec(num_scalar_...  13.8 us
    all_to_all x1, starting transfers between devices, on_device(): lax.all_to_all(by_head, 'tp', split_axis=0, concat_axis=0, tiled=True)  11.6 us
    all_to_all x1, starting transfers between devices, on_device(): lax.all_to_all(to_send, 'req', split_axis=0, concat_axis=0, tiled=True)  11.5 us
    ppermute x7, starting transfers between devices, share_over_req(): lax.ppermute(known, 'req', [(d, d ^ step) for d in range(groups)])  7.92 us
    ppermute x7, waiting for transfers between devices, share_over_req(): lax.ppermute(known, 'req', [(d, d ^ step) for d in range(groups)])  6.01 us
  transfers between devices with their start and end apart: 9, of which 6 were waited for; matrix products, arithmetic and copies ran while one was open for 1% of the time, Pallas kernels for 13%

profile of v4, /device:TPU:1, one launch (start us, length us, event | category | flops | bytes accessed | tf_op | source)
XLA Modules:
  0.0 107.4 jit_solution(8905626315763453708)
XLA Ops:
  0.0 1.9 %copy.16 = bf16[2,8,8,8,256]{4,3,1,0,2:T(8,128)(2,1)} copy(bf16[2,8,8,8,256]{4,3,2,1,0:T(8,128)(2,1)} %bitcast.16) | data formatting | bytes 1048576 | tf_op jit(solution)/shard_map/reshape | solution.py:288
  1.9 11.6 %all-to-all-start = ((bf16[8,2,64,256]{3,2,1,0:T(8,128)(2,1)}), bf16[8,2,64,256]{3,2,1,0:T(8,128)(2,1)S(1)}, u32[]{:S(2)}, u32[]{:S(2)}) async-start(bf16[8,2,64,256]{3,2,1,0:T(8,128)(2,1)} %bitcast.14), calls=%async_computation | async-start | bytes 1048576 | tf_op jit(solution)/shard_map/all_to_all | solution.py:289
  13.8 0.2 select_reduce_fusion
  14.0 1.0 collective-permute-start
  15.1 0.8 collective-permute-done
  15.9 2.5 %collective-permute-start.3 = (s32[2,32]{1,0:T(2,128)S(1)}, s32[2,32]{1,0:T(2,128)S(1)}, u32[]{:S(2)}, u32[]{:S(2)}) collective-permute-start(s32[2,32]{1,0:T(2,128)S(1)} %pad_add_fusion), channel_id=1, source_target_pairs={{0,48},{8,56},{16,32},{24,40},{32,16},{40,24},{48,0},{56,8},{64,11... | collective-permute-start | bytes 776 | tf_op jit(solution)/shard_map/ppermute | solution.py:265
  18.4 0.5 collective-permute-start.2
  18.9 0.3 collective-permute-start.1
  19.2 0.7 collective-permute-done.3
  19.8 2.8 %collective-permute-done.2 = s32[2,32]{1,0:T(2,128)S(1)} collective-permute-done((s32[2,32]{1,0:T(2,128)S(1)}, s32[2,32]{1,0:T(2,128)S(1)}, u32[]{:S(2)}, u32[]{:S(2)}) %collective-permute-start.2) | collective-permute-done | bytes 288 | tf_op jit(solution)/shard_map/ppermute | solution.py:265
  22.6 1.7 %collective-permute-start.6 = (s32[8,32]{1,0:T(8,128)S(1)}, s32[8,32]{1,0:T(8,128)S(1)}, u32[]{:S(2)}, u32[]{:S(2)}) collective-permute-start(s32[8,32]{1,0:T(8,128)S(1)} %concatenate.12), channel_id=1, source_target_pairs={{0,192},{8,200},{16,208},{24,216},{32,224},{40,232},{48,240},{56,2... | collective-permute-start | bytes 3080 | tf_op jit(solution)/shard_map/ppermute | solution.py:265
  24.4 1.9 %collective-permute-start.4 = (s32[8,32]{1,0:T(8,128)S(1)}, s32[8,32]{1,0:T(8,128)S(1)}, u32[]{:S(2)}, u32[]{:S(2)}) collective-permute-start(s32[8,32]{1,0:T(8,128)S(1)} %concatenate.12), channel_id=1, source_target_pairs={{0,64},{8,72},{16,80},{24,88},{32,96},{40,104},{48,112},{56,120},{... | collective-permute-start | bytes 3080 | tf_op jit(solution)/shard_map/ppermute | solution.py:265
  26.3 1.0 collective-permute-done.6
  27.3 0.7 collective-permute-done.5
  28.0 0.1 select_reduce_fusion.2
  28.2 0.1 copy.12
  28.3 0.1 reshape.157.wanted_ref
  28.4 1.9 %pick_blocks.1 = bf16[64,64,256]{2,1,0:T(8,128)(2,1)} custom-call(s32[64]{0:T(128)S(1)} %reshape.157.wanted_ref, s32[1]{0:T(128)} %bitcast.3.me_ref, bf16[16,64,256]{2,1,0:T(8,128)(2,1)S(1)} %bitcast.15), custom_call_target="tpu_custom_call" | custom-call | tf_op jit(solution)/shard_map/pick_blocks/pallas_call | solution.py:49
  30.4 11.5 %all-to-all-start.1 = ((bf16[64,64,256]{2,1,0:T(8,128)(2,1)}), bf16[64,64,256]{2,1,0:T(8,128)(2,1)}, u32[]{:S(2)}, u32[]{:S(2)}) async-start(bf16[64,64,256]{2,1,0:T(8,128)(2,1)} %pick_blocks.1), calls=%async_computation.1 | async-start | bytes 4194304 | tf_op jit(solution)/shard_map/all_to_all | solution.py:292
  41.9 0.2 and_reduce_fusion
  42.2 13.8 %fresh_attention.1 = (f32[1024,1024]{1,0:T(8,128)}, f32[4,1024,128]{2,1,0:T(8,128)S(1)}, f32[4]{0:T(128)S(1)}) custom-call(s32[2]{0:T(128)S(1)} %copy-done.2, bf16[1024,1024]{1,0:T(8,128)(2,1)} %q_any.1, bf16[1024,256]{1,0:T(8,128)(2,1)S(1)} %copy-done.1), custom_call_target="tpu_custom_call" | custom-call | flops 4294967296 | bytes 12582912 | tf_op jit(solution)/shard_map/fresh_attention/pallas_call | solution.py:106
  55.9 1.3 %copy-done.4 = f32[4,1024,128]{2,1,0:T(8,128)} copy-done((f32[4,1024,128]{2,1,0:T(8,128)}, f32[4,1024,128]{2,1,0:T(8,128)S(1)}, u32[]{:S(2)}) %copy-start.4) | copy-done | bytes 2097176
  57.3 32.7 %all-to-all-done.1.recv_any = bf16[64,64,256]{2,1,0:T(8,128)(2,1)} async-done(((bf16[64,64,256]{2,1,0:T(8,128)(2,1)}), bf16[64,64,256]{2,1,0:T(8,128)(2,1)}, u32[]{:S(2)}, u32[]{:S(2)}) %all-to-all-start.1) | async-done | bytes 2097184 | tf_op jit(solution)/shard_map/all_to_all | solution.py:292
  90.0 17.2 %prefix_attention.1 = bf16[1024,1024]{1,0:T(8,128)(2,1)} custom-call(s32[2]{0:T(128)S(1)} %copy-done.2, s32[32]{0:T(128)S(1)} %add_select_fusion.place_ref, s32[2]{0:T(128)S(1)} %copy-done.3, f32[4]{0:T(128)S(1)} %get-tuple-element.8.excess_ref, bf16[1024,1024]{1,0:T(8,128)(2,1)S(1)} %copy-done, bf16[64,64,256]{2,1,0:T(8,128)(2,1)} %all-to-all-done.1.recv_any, ...), custom_call_target="tpu_custom_call" | custom-call | flops 4294967296 | bytes 12582912 | tf_op jit(solution)/shard_map/prefix_attention/pallas_call | solution.py:229
  (30 shorter events, 0.5 us)
Async XLA Ops:
  0.0 13.6 %copy-start.3 = (s32[2]{0:T(128)S(1)}, s32[2]{0:T(128)}, u32[]{:S(2)}) copy-start(s32[2]{0:T(128)} %count_ref.1) | copy-start | bytes 28
  0.0 13.7 %copy-start.6 = (s32[2,16]{1,0:T(2,128)S(1)}, s32[2,16]{1,0:T(2,128)}, u32[]{:S(2)}) copy-start(s32[2,16]{1,0:T(2,128)} %param.11) | copy-start | bytes 388
  0.0 13.8 %copy-start.5 = (s32[512]{0:T(512)S(1)}, s32[512]{0:T(512)}, u32[]{:S(2)}) copy-start(s32[512]{0:T(512)} %param.13) | copy-start | bytes 6148
  1.9 26.4 %all-to-all-start = ((bf16[8,2,64,256]{3,2,1,0:T(8,128)(2,1)}), bf16[8,2,64,256]{3,2,1,0:T(8,128)(2,1)S(1)}, u32[]{:S(2)}, u32[]{:S(2)}) async-start(bf16[8,2,64,256]{3,2,1,0:T(8,128)(2,1)} %bitcast.14), calls=%async_computation | async-start | bytes 1048576 | tf_op jit(solution)/shard_map/all_to_all | solution.py:289
  14.0 1.9 %collective-permute-start = (s32[1,32]{1,0:T(1,128)S(1)}, s32[1,32]{1,0:T(1,128)S(1)}, u32[]{:S(2)}, u32[]{:S(2)}) collective-permute-start(s32[1,32]{1,0:T(1,128)S(1)} %bitcast_select_fusion), channel_id=1, source_target_pairs={{0,8},{8,0},{16,24},{24,16},{32,40},{40,32},{48,56},{56,48},{64,72... | collective-permute-start | bytes 392 | tf_op jit(solution)/shard_map/ppermute | solution.py:265
  15.9 3.9 %collective-permute-start.3 = (s32[2,32]{1,0:T(2,128)S(1)}, s32[2,32]{1,0:T(2,128)S(1)}, u32[]{:S(2)}, u32[]{:S(2)}) collective-permute-start(s32[2,32]{1,0:T(2,128)S(1)} %pad_add_fusion), channel_id=1, source_target_pairs={{0,48},{8,56},{16,32},{24,40},{32,16},{40,24},{48,0},{56,8},{64,11... | collective-permute-start | bytes 776 | tf_op jit(solution)/shard_map/ppermute | solution.py:265
  18.4 4.2 %collective-permute-start.2 = (s32[2,32]{1,0:T(2,128)S(1)}, s32[2,32]{1,0:T(2,128)S(1)}, u32[]{:S(2)}, u32[]{:S(2)}) collective-permute-start(s32[2,32]{1,0:T(2,128)S(1)} %pad_add_fusion), channel_id=1, source_target_pairs={{0,32},{8,40},{16,48},{24,56},{32,0},{40,8},{48,16},{56,24},{64,96... | collective-permute-start | bytes 776 | tf_op jit(solution)/shard_map/ppermute | solution.py:265
  18.9 3.7 %collective-permute-start.1 = (s32[2,32]{1,0:T(2,128)S(1)}, s32[2,32]{1,0:T(2,128)S(1)}, u32[]{:S(2)}, u32[]{:S(2)}) collective-permute-start(s32[2,32]{1,0:T(2,128)S(1)} %pad_add_fusion), channel_id=1, source_target_pairs={{0,16},{8,24},{16,0},{24,8},{32,48},{40,56},{48,32},{56,40},{64,80... | collective-permute-start | bytes 776 | tf_op jit(solution)/shard_map/ppermute | solution.py:265
  22.6 4.6 %collective-permute-start.6 = (s32[8,32]{1,0:T(8,128)S(1)}, s32[8,32]{1,0:T(8,128)S(1)}, u32[]{:S(2)}, u32[]{:S(2)}) collective-permute-start(s32[8,32]{1,0:T(8,128)S(1)} %concatenate.12), channel_id=1, source_target_pairs={{0,192},{8,200},{16,208},{24,216},{32,224},{40,232},{48,240},{56,2... | collective-permute-start | bytes 3080 | tf_op jit(solution)/shard_map/ppermute | solution.py:265
  24.3 3.7 %collective-permute-start.5 = (s32[8,32]{1,0:T(8,128)S(1)}, s32[8,32]{1,0:T(8,128)S(1)}, u32[]{:S(2)}, u32[]{:S(2)}) collective-permute-start(s32[8,32]{1,0:T(8,128)S(1)} %concatenate.12), channel_id=1, source_target_pairs={{0,128},{8,136},{16,144},{24,152},{32,160},{40,168},{48,176},{56,1... | collective-permute-start | bytes 3080 | tf_op jit(solution)/shard_map/ppermute | solution.py:265
  24.4 3.7 %collective-permute-start.4 = (s32[8,32]{1,0:T(8,128)S(1)}, s32[8,32]{1,0:T(8,128)S(1)}, u32[]{:S(2)}, u32[]{:S(2)}) collective-permute-start(s32[8,32]{1,0:T(8,128)S(1)} %concatenate.12), channel_id=1, source_target_pairs={{0,64},{8,72},{16,80},{24,88},{32,96},{40,104},{48,112},{56,120},{... | collective-permute-start | bytes 3080 | tf_op jit(solution)/shard_map/ppermute | solution.py:265
  30.3 11.8 %copy-start.1 = (bf16[1024,256]{1,0:T(8,128)(2,1)S(1)}, bf16[1024,256]{1,0:T(8,128)(2,1)}, u32[]{:S(2)}) copy-start(bf16[1024,256]{1,0:T(8,128)(2,1)} %kv_ref.1) | copy-start | bytes 1572868
  30.3 11.8 %copy-start.2 = (s32[2]{0:T(128)S(1)}, s32[2]{0:T(128)}, u32[]{:S(2)}) copy-start(s32[2]{0:T(128)} %owner_ref.3) | copy-start | bytes 28
  30.4 59.6 %all-to-all-start.1 = ((bf16[64,64,256]{2,1,0:T(8,128)(2,1)}), bf16[64,64,256]{2,1,0:T(8,128)(2,1)}, u32[]{:S(2)}, u32[]{:S(2)}) async-start(bf16[64,64,256]{2,1,0:T(8,128)(2,1)} %pick_blocks.1), calls=%async_computation.1 | async-start | bytes 4194304 | tf_op jit(solution)/shard_map/all_to_all | solution.py:292
  42.2 47.9 %copy-start = (bf16[1024,1024]{1,0:T(8,128)(2,1)S(1)}, bf16[1024,1024]{1,0:T(8,128)(2,1)}, u32[]{:S(2)}) copy-start(bf16[1024,1024]{1,0:T(8,128)(2,1)} %q_any.1) | copy-start | bytes 6291460
  55.9 1.3 %copy-start.4 = (f32[4,1024,128]{2,1,0:T(8,128)}, f32[4,1024,128]{2,1,0:T(8,128)S(1)}, u32[]{:S(2)}) copy-start(f32[4,1024,128]{2,1,0:T(8,128)S(1)} %get-tuple-element.10.stat_any) | copy-start | bytes 6291460

commit v5 on v4

--- a/solution.py
+++ b/solution.py
@@ -142,8 +142,8 @@
     sure = MIN_LIVE * PB
 
     def kernel(
-        owner_ref, place_ref, count_ref, excess_ref, q_any, recv_any, acc_any, stat_any, out_any,
-        kv_scr, v_scr, q_scr, acc_scr, stat_scr, out_scr, kv_sem, in_sem, out_sem,
+        owner_ref, place_ref, count_ref, excess_ref, q_ref, recv_any, acc_any, stat_any, out_any,
+        kv_scr, v_scr, acc_scr, stat_scr, out_scr, kv_sem, in_sem, out_sem,
     ):
         def kv_copy(i):
             request, to = i // PREF, pl.ds(pl.multiple_of((i % PREF) * PB, PB), PB)
@@ -160,9 +160,8 @@
         def in_copies(step):
             column = pl.ds(pl.multiple_of(step * step_width, step_width), step_width)
             return (
-                pltpu.make_async_copy(q_any.at[:, column], q_scr.at[step], in_sem.at[step, 0]),
-                pltpu.make_async_copy(acc_any.at[:, column], acc_scr.at[step], in_sem.at[step, 1]),
-                pltpu.make_async_copy(stat_any.at[step], stat_scr.at[step], in_sem.at[step, 2]),
+                pltpu.make_async_copy(acc_any.at[:, column], acc_scr.at[step], in_sem.at[step, 0]),
+                pltpu.make_async_copy(stat_any.at[step], stat_scr.at[step], in_sem.at[step, 1]),
             )
 
         def out_copy(step):
@@ -179,12 +178,13 @@
         def attend(step, with_maximum):
             for part in range(HEAD_STEP):
                 column = slice(part * HD, (part + 1) * HD)
+                q_column = pl.ds(pl.multiple_of((step * HEAD_STEP + part) * HD, HD), HD)
                 for slot in range(slots):
                     owner = owner_ref[slot]
                     live = count_ref[owner] * PB
                     for first in range(slot * span, (slot + 1) * span, ROW_TILE):
                         tile = slice(first, first + ROW_TILE)
-                        s = scores_of(q_scr[step, tile, column], kv_scr[owner, :, :HD])
+                        s = scores_of(q_ref[tile, q_column], kv_scr[owner, :, :HD])
                         key = sure + lax.broadcasted_iota(jnp.int32, (ROW_TILE, keys - sure), 1)
                         s = jnp.concatenate([s[:, :sure], jnp.where(key < live, s[:, sure:], MASKED)], axis=1)
                         top = stat_scr[step, tile, 2 * part : 2 * part + 1]
@@ -228,17 +228,16 @@
     smem, anywhere = pl.BlockSpec(memory_space=pltpu.SMEM), pl.BlockSpec(memory_space=pl.ANY)
     return pl.pallas_call(
         kernel,
-        in_specs=[smem] * 4 + [anywhere] * 4,
+        in_specs=[smem] * 4 + [pl.BlockSpec(memory_space=pltpu.VMEM)] + [anywhere] * 3,
         out_specs=anywhere,
         scratch_shapes=[
             pltpu.VMEM((REQ_DEV, keys, 2 * HD), jnp.bfloat16),
             pltpu.VMEM((REQ_DEV, keys, 2 * HD), jnp.bfloat16),
-            pltpu.VMEM((steps, rows, step_width), jnp.bfloat16),
             pltpu.VMEM((steps, rows, step_width), jnp.float32),
             pltpu.VMEM((steps, rows, HD), jnp.float32),
             pltpu.VMEM((steps, rows, step_width), jnp.bfloat16),
             pltpu.SemaphoreType.DMA((REQ_DEV * PREF,)),
-            pltpu.SemaphoreType.DMA((steps, 3)),
+            pltpu.SemaphoreType.DMA((steps, 2)),
             pltpu.SemaphoreType.DMA((steps,)),
         ],
         out_shape=jax.ShapeDtypeStruct((rows, width), jnp.bfloat16),

time: 108 us -> 108 us (level)
  no operation moved by 1% of the time
where the time goes in v5:
time: 108 us; the launch traced here: 107 us
  waiting for transfers between devices  38.8 us (36%)
  Pallas kernels  32.8 us (30%)
  starting transfers between devices  31 us (29%)
  local copies, waits for them, and re-layouts  3.79 us (4%)
    all_to_all x1, waiting for transfers between devices, on_device(): lax.all_to_all(to_send, 'req', split_axis=0, concat_axis=0, tiled=True)  32.7 us
    pallas_call x1, Pallas kernels, prefix_attention(): pl.pallas_call(kernel, in_specs=[smem] * 4 + [pl.BlockSpec(memory_space=p...  17.1 us
    pallas_call x1, Pallas kernels, fresh_attention(): pl.pallas_call(kernel, grid_spec=pltpu.PrefetchScalarGridSpec(num_scalar_...  13.8 us
    all_to_all x1, starting transfers between devices, on_device(): lax.all_to_all(by_head, 'tp', split_axis=0, concat_axis=0, tiled=True)  11.6 us
    all_to_all x1, starting transfers between devices, on_device(): lax.all_to_all(to_send, 'req', split_axis=0, concat_axis=0, tiled=True)  11.5 us
    ppermute x7, starting transfers between devices, share_over_req(): lax.ppermute(known, 'req', [(d, d ^ step) for d in range(groups)])  7.92 us
    ppermute x7, waiting for transfers between devices, share_over_req(): lax.ppermute(known, 'req', [(d, d ^ step) for d in range(groups)])  6.01 us
  transfers between devices with their start and end apart: 9, of which 6 were waited for; matrix products, arithmetic and copies ran while one was open for 1% of the time, Pallas kernels for 13%

profile of v5, /device:TPU:1, one launch (start us, length us, event | category | flops | bytes accessed | tf_op | source)
XLA Modules:
  0.0 107.3 jit_solution(11887141471314402886)
XLA Ops:
  0.0 1.9 %copy.16 = bf16[2,8,8,8,256]{4,3,1,0,2:T(8,128)(2,1)} copy(bf16[2,8,8,8,256]{4,3,2,1,0:T(8,128)(2,1)} %bitcast.16) | data formatting | bytes 1048576 | tf_op jit(solution)/shard_map/reshape | solution.py:287
  1.9 11.6 %all-to-all-start = ((bf16[8,2,64,256]{3,2,1,0:T(8,128)(2,1)}), bf16[8,2,64,256]{3,2,1,0:T(8,128)(2,1)S(1)}, u32[]{:S(2)}, u32[]{:S(2)}) async-start(bf16[8,2,64,256]{3,2,1,0:T(8,128)(2,1)} %bitcast.14), calls=%async_computation | async-start | bytes 1048576 | tf_op jit(solution)/shard_map/all_to_all | solution.py:288
  13.8 0.2 select_reduce_fusion
  14.0 1.0 collective-permute-start
  15.1 0.8 collective-permute-done
  15.9 2.5 %collective-permute-start.3 = (s32[2,32]{1,0:T(2,128)S(1)}, s32[2,32]{1,0:T(2,128)S(1)}, u32[]{:S(2)}, u32[]{:S(2)}) collective-permute-start(s32[2,32]{1,0:T(2,128)S(1)} %pad_add_fusion), channel_id=1, source_target_pairs={{0,48},{8,56},{16,32},{24,40},{32,16},{40,24},{48,0},{56,8},{64,11... | collective-permute-start | bytes 776 | tf_op jit(solution)/shard_map/ppermute | solution.py:264
  18.4 0.5 collective-permute-start.2
  18.9 0.3 collective-permute-start.1
  19.2 0.7 collective-permute-done.3
  19.8 2.8 %collective-permute-done.2 = s32[2,32]{1,0:T(2,128)S(1)} collective-permute-done((s32[2,32]{1,0:T(2,128)S(1)}, s32[2,32]{1,0:T(2,128)S(1)}, u32[]{:S(2)}, u32[]{:S(2)}) %collective-permute-start.2) | collective-permute-done | bytes 288 | tf_op jit(solution)/shard_map/ppermute | solution.py:264
  22.6 1.7 %collective-permute-start.6 = (s32[8,32]{1,0:T(8,128)S(1)}, s32[8,32]{1,0:T(8,128)S(1)}, u32[]{:S(2)}, u32[]{:S(2)}) collective-permute-start(s32[8,32]{1,0:T(8,128)S(1)} %concatenate.12), channel_id=1, source_target_pairs={{0,192},{8,200},{16,208},{24,216},{32,224},{40,232},{48,240},{56,2... | collective-permute-start | bytes 3080 | tf_op jit(solution)/shard_map/ppermute | solution.py:264
  24.4 1.9 %collective-permute-start.4 = (s32[8,32]{1,0:T(8,128)S(1)}, s32[8,32]{1,0:T(8,128)S(1)}, u32[]{:S(2)}, u32[]{:S(2)}) collective-permute-start(s32[8,32]{1,0:T(8,128)S(1)} %concatenate.12), channel_id=1, source_target_pairs={{0,64},{8,72},{16,80},{24,88},{32,96},{40,104},{48,112},{56,120},{... | collective-permute-start | bytes 3080 | tf_op jit(solution)/shard_map/ppermute | solution.py:264
  26.3 1.0 collective-permute-done.6
  27.3 0.7 collective-permute-done.5
  28.0 0.1 select_reduce_fusion.2
  28.2 0.1 copy.12
  28.3 0.1 reshape.157.wanted_ref
  28.4 1.9 %pick_blocks.1 = bf16[64,64,256]{2,1,0:T(8,128)(2,1)} custom-call(s32[64]{0:T(128)S(1)} %reshape.157.wanted_ref, s32[1]{0:T(128)} %bitcast.3.me_ref, bf16[16,64,256]{2,1,0:T(8,128)(2,1)S(1)} %bitcast.15), custom_call_target="tpu_custom_call" | custom-call | tf_op jit(solution)/shard_map/pick_blocks/pallas_call | solution.py:49
  30.4 11.5 %all-to-all-start.1 = ((bf16[64,64,256]{2,1,0:T(8,128)(2,1)}), bf16[64,64,256]{2,1,0:T(8,128)(2,1)}, u32[]{:S(2)}, u32[]{:S(2)}) async-start(bf16[64,64,256]{2,1,0:T(8,128)(2,1)} %pick_blocks.1), calls=%async_computation.1 | async-start | bytes 4194304 | tf_op jit(solution)/shard_map/all_to_all | solution.py:291
  41.9 0.2 and_reduce_fusion
  42.2 13.8 %fresh_attention.1 = (f32[1024,1024]{1,0:T(8,128)}, f32[4,1024,128]{2,1,0:T(8,128)S(1)}, f32[4]{0:T(128)S(1)}) custom-call(s32[2]{0:T(128)S(1)} %copy-done.2, bf16[1024,1024]{1,0:T(8,128)(2,1)} %q_ref.3, bf16[1024,256]{1,0:T(8,128)(2,1)S(1)} %copy-done.1), custom_call_target="tpu_custom_call" | custom-call | flops 4294967296 | bytes 12582912 | tf_op jit(solution)/shard_map/fresh_attention/pallas_call | solution.py:106
  55.9 1.3 %copy-done.4 = f32[4,1024,128]{2,1,0:T(8,128)} copy-done((f32[4,1024,128]{2,1,0:T(8,128)}, f32[4,1024,128]{2,1,0:T(8,128)S(1)}, u32[]{:S(2)}) %copy-start.4) | copy-done | bytes 2097176
  57.3 32.7 %all-to-all-done.1.recv_any = bf16[64,64,256]{2,1,0:T(8,128)(2,1)} async-done(((bf16[64,64,256]{2,1,0:T(8,128)(2,1)}), bf16[64,64,256]{2,1,0:T(8,128)(2,1)}, u32[]{:S(2)}, u32[]{:S(2)}) %all-to-all-start.1) | async-done | bytes 2097184 | tf_op jit(solution)/shard_map/all_to_all | solution.py:291
  90.0 17.1 %prefix_attention.1 = bf16[1024,1024]{1,0:T(8,128)(2,1)} custom-call(s32[2]{0:T(128)S(1)} %copy-done.2, s32[32]{0:T(128)S(1)} %add_select_fusion.place_ref, s32[2]{0:T(128)S(1)} %copy-done.3, f32[4]{0:T(128)S(1)} %get-tuple-element.8.excess_ref, bf16[1024,1024]{1,0:T(8,128)(2,1)S(1)} %copy-done, bf16[64,64,256]{2,1,0:T(8,128)(2,1)} %all-to-all-done.1.recv_any, ...), custom_call_target="tpu_custom_call" | custom-call | flops 4294967296 | bytes 12582912 | tf_op jit(solution)/shard_map/prefix_attention/pallas_call | solution.py:229
  (30 shorter events, 0.5 us)
Async XLA Ops:
  0.0 13.6 %copy-start.3 = (s32[2]{0:T(128)S(1)}, s32[2]{0:T(128)}, u32[]{:S(2)}) copy-start(s32[2]{0:T(128)} %count_ref.1) | copy-start | bytes 28
  0.0 13.7 %copy-start.6 = (s32[2,16]{1,0:T(2,128)S(1)}, s32[2,16]{1,0:T(2,128)}, u32[]{:S(2)}) copy-start(s32[2,16]{1,0:T(2,128)} %param.11) | copy-start | bytes 388
  0.0 13.8 %copy-start.5 = (s32[512]{0:T(512)S(1)}, s32[512]{0:T(512)}, u32[]{:S(2)}) copy-start(s32[512]{0:T(512)} %param.13) | copy-start | bytes 6148
  1.9 26.4 %all-to-all-start = ((bf16[8,2,64,256]{3,2,1,0:T(8,128)(2,1)}), bf16[8,2,64,256]{3,2,1,0:T(8,128)(2,1)S(1)}, u32[]{:S(2)}, u32[]{:S(2)}) async-start(bf16[8,2,64,256]{3,2,1,0:T(8,128)(2,1)} %bitcast.14), calls=%async_computation | async-start | bytes 1048576 | tf_op jit(solution)/shard_map/all_to_all | solution.py:288
  14.0 1.9 %collective-permute-start = (s32[1,32]{1,0:T(1,128)S(1)}, s32[1,32]{1,0:T(1,128)S(1)}, u32[]{:S(2)}, u32[]{:S(2)}) collective-permute-start(s32[1,32]{1,0:T(1,128)S(1)} %bitcast_select_fusion), channel_id=1, source_target_pairs={{0,8},{8,0},{16,24},{24,16},{32,40},{40,32},{48,56},{56,48},{64,72... | collective-permute-start | bytes 392 | tf_op jit(solution)/shard_map/ppermute | solution.py:264
  15.9 3.9 %collective-permute-start.3 = (s32[2,32]{1,0:T(2,128)S(1)}, s32[2,32]{1,0:T(2,128)S(1)}, u32[]{:S(2)}, u32[]{:S(2)}) collective-permute-start(s32[2,32]{1,0:T(2,128)S(1)} %pad_add_fusion), channel_id=1, source_target_pairs={{0,48},{8,56},{16,32},{24,40},{32,16},{40,24},{48,0},{56,8},{64,11... | collective-permute-start | bytes 776 | tf_op jit(solution)/shard_map/ppermute | solution.py:264
  18.4 4.2 %collective-permute-start.2 = (s32[2,32]{1,0:T(2,128)S(1)}, s32[2,32]{1,0:T(2,128)S(1)}, u32[]{:S(2)}, u32[]{:S(2)}) collective-permute-start(s32[2,32]{1,0:T(2,128)S(1)} %pad_add_fusion), channel_id=1, source_target_pairs={{0,32},{8,40},{16,48},{24,56},{32,0},{40,8},{48,16},{56,24},{64,96... | collective-permute-start | bytes 776 | tf_op jit(solution)/shard_map/ppermute | solution.py:264
  18.9 3.7 %collective-permute-start.1 = (s32[2,32]{1,0:T(2,128)S(1)}, s32[2,32]{1,0:T(2,128)S(1)}, u32[]{:S(2)}, u32[]{:S(2)}) collective-permute-start(s32[2,32]{1,0:T(2,128)S(1)} %pad_add_fusion), channel_id=1, source_target_pairs={{0,16},{8,24},{16,0},{24,8},{32,48},{40,56},{48,32},{56,40},{64,80... | collective-permute-start | bytes 776 | tf_op jit(solution)/shard_map/ppermute | solution.py:264
  22.6 4.6 %collective-permute-start.6 = (s32[8,32]{1,0:T(8,128)S(1)}, s32[8,32]{1,0:T(8,128)S(1)}, u32[]{:S(2)}, u32[]{:S(2)}) collective-permute-start(s32[8,32]{1,0:T(8,128)S(1)} %concatenate.12), channel_id=1, source_target_pairs={{0,192},{8,200},{16,208},{24,216},{32,224},{40,232},{48,240},{56,2... | collective-permute-start | bytes 3080 | tf_op jit(solution)/shard_map/ppermute | solution.py:264
  24.3 3.7 %collective-permute-start.5 = (s32[8,32]{1,0:T(8,128)S(1)}, s32[8,32]{1,0:T(8,128)S(1)}, u32[]{:S(2)}, u32[]{:S(2)}) collective-permute-start(s32[8,32]{1,0:T(8,128)S(1)} %concatenate.12), channel_id=1, source_target_pairs={{0,128},{8,136},{16,144},{24,152},{32,160},{40,168},{48,176},{56,1... | collective-permute-start | bytes 3080 | tf_op jit(solution)/shard_map/ppermute | solution.py:264
  24.4 3.7 %collective-permute-start.4 = (s32[8,32]{1,0:T(8,128)S(1)}, s32[8,32]{1,0:T(8,128)S(1)}, u32[]{:S(2)}, u32[]{:S(2)}) collective-permute-start(s32[8,32]{1,0:T(8,128)S(1)} %concatenate.12), channel_id=1, source_target_pairs={{0,64},{8,72},{16,80},{24,88},{32,96},{40,104},{48,112},{56,120},{... | collective-permute-start | bytes 3080 | tf_op jit(solution)/shard_map/ppermute | solution.py:264
  30.3 11.8 %copy-start.1 = (bf16[1024,256]{1,0:T(8,128)(2,1)S(1)}, bf16[1024,256]{1,0:T(8,128)(2,1)}, u32[]{:S(2)}) copy-start(bf16[1024,256]{1,0:T(8,128)(2,1)} %kv_ref.1) | copy-start | bytes 1572868
  30.3 11.8 %copy-start.2 = (s32[2]{0:T(128)S(1)}, s32[2]{0:T(128)}, u32[]{:S(2)}) copy-start(s32[2]{0:T(128)} %owner_ref.3) | copy-start | bytes 28
  30.4 59.6 %all-to-all-start.1 = ((bf16[64,64,256]{2,1,0:T(8,128)(2,1)}), bf16[64,64,256]{2,1,0:T(8,128)(2,1)}, u32[]{:S(2)}, u32[]{:S(2)}) async-start(bf16[64,64,256]{2,1,0:T(8,128)(2,1)} %pick_blocks.1), calls=%async_computation.1 | async-start | bytes 4194304 | tf_op jit(solution)/shard_map/all_to_all | solution.py:291
  42.2 47.9 %copy-start = (bf16[1024,1024]{1,0:T(8,128)(2,1)S(1)}, bf16[1024,1024]{1,0:T(8,128)(2,1)}, u32[]{:S(2)}) copy-start(bf16[1024,1024]{1,0:T(8,128)(2,1)} %q_ref.3) | copy-start | bytes 6291460
  55.9 1.3 %copy-start.4 = (f32[4,1024,128]{2,1,0:T(8,128)}, f32[4,1024,128]{2,1,0:T(8,128)S(1)}, u32[]{:S(2)}) copy-start(f32[4,1024,128]{2,1,0:T(8,128)S(1)} %get-tuple-element.10.stat_any) | copy-start | bytes 6291460

commit v6 on v5

--- a/solution.py
+++ b/solution.py
@@ -24,6 +24,26 @@
 FRESH_VMEM_LIMIT = 51712 * 1024
 PREFIX_VMEM_LIMIT = 51712 * 1024
 PICK_VMEM_LIMIT = 8 * 1024 * 1024
+LAY_VMEM_LIMIT = 60 * 1024 * 1024
+
+
+def lay_by_head(pool_kv, head_width):
+    blocks, tokens, columns = pool_kv.shape
+    heads = columns // head_width
+
+    def kernel(pool_ref, out_ref):
+        for head in range(heads):
+            out_ref[head, 0] = pool_ref[0, :, head * head_width : (head + 1) * head_width]
+
+    return pl.pallas_call(
+        kernel,
+        grid=(blocks,),
+        in_specs=[pl.BlockSpec((1, tokens, columns), lambda i: (i, 0, 0))],
+        out_specs=pl.BlockSpec((heads, 1, tokens, head_width), lambda i: (0, i, 0, 0)),
+        out_shape=jax.ShapeDtypeStruct((heads, blocks, tokens, head_width), pool_kv.dtype),
+        compiler_params=pltpu.CompilerParams(vmem_limit_bytes=LAY_VMEM_LIMIT),
+        name="lay_by_head",
+    )(pool_kv)
 
 
 def pick_blocks(wanted, me, group_store):
@@ -284,7 +304,7 @@
     rows = used_rows(prefix_ids, prefix_count, block_row)
     low, high = low_high(share_over_req(rows), me * group_rows, group_rows)
     wanted = jnp.stack([low, high], axis=1).reshape(-1)
-    by_head = pool_kv.reshape(pool_local, PB, tp_count, head_width).transpose(2, 0, 1, 3)
+    by_head = lay_by_head(pool_kv, head_width)
     group_store = lax.all_to_all(by_head, "tp", split_axis=0, concat_axis=0, tiled=True)
     group_store = group_store.reshape(group_rows, PB, head_width)
     to_send = pick_blocks(wanted, me[None], group_store)

time: 108 us -> 109 us (level)
  Pallas kernels: 32.8 us -> 36.1 us
  local copies, waits for them, and re-layouts: 3.79 us -> 1.87 us
    reshape x1 -> x0, local copies, waits for them, and re-layouts: 1.92 us -> none  [on_device(): pool_kv.reshape(pool_local, PB, tp_count, head_width).transpose(2, 0, 1, 3)]
    pallas_call x0 -> x1, Pallas kernels: none -> 1.79 us  [lay_by_head(): pl.pallas_call(kernel, grid=(blocks,), in_specs=[pl.BlockSpec((1, tokens,...]
    pallas_call x1, Pallas kernels: 17.1 us -> 18.6 us  [prefix_attention(): pl.pallas_call(kernel, in_specs=[smem] * 4 + [pl.BlockSpec(memory_space=p...]
where the time goes in v6:
time: 109 us
  waiting for transfers between devices  38.7 us (36%)
  Pallas kernels  36.1 us (33%)
  starting transfers between devices  31 us (28%)
  local copies, waits for them, and re-layouts  1.87 us (2%)
    all_to_all x1, waiting for transfers between devices, on_device(): lax.all_to_all(to_send, 'req', split_axis=0, concat_axis=0, tiled=True)  32.6 us
    pallas_call x1, Pallas kernels, prefix_attention(): pl.pallas_call(kernel, in_specs=[smem] * 4 + [pl.BlockSpec(memory_space=p...  18.6 us
    pallas_call x1, Pallas kernels, fresh_attention(): pl.pallas_call(kernel, grid_spec=pltpu.PrefetchScalarGridSpec(num_scalar_...  13.8 us
    all_to_all x1, starting transfers between devices, on_device(): lax.all_to_all(by_head, 'tp', split_axis=0, concat_axis=0, tiled=True)  11.6 us
    all_to_all x1, starting transfers between devices, on_device(): lax.all_to_all(to_send, 'req', split_axis=0, concat_axis=0, tiled=True)  11.5 us
    ppermute x7, starting transfers between devices, share_over_req(): lax.ppermute(known, 'req', [(d, d ^ step) for d in range(groups)])  7.92 us
    ppermute x7, waiting for transfers between devices, share_over_req(): lax.ppermute(known, 'req', [(d, d ^ step) for d in range(groups)])  6.01 us
  transfers between devices with their start and end apart: 9, of which 6 were waited for; matrix products, arithmetic and copies ran while one was open for 1% of the time, Pallas kernels for 13%

profile of v6, /device:TPU:1, one launch (start us, length us, event | category | flops | bytes accessed | tf_op | source)
XLA Modules:
  0.0 108.6 jit_solution(15046502774432689294)
XLA Ops:
  0.0 1.8 %lay_by_head.1 = bf16[8,2,64,256]{3,2,1,0:T(8,128)(2,1)} custom-call(bf16[2,64,2048]{2,1,0:T(8,128)(2,1)} %pool_ref.1), custom_call_target="tpu_custom_call" | custom-call | tf_op jit(solution)/shard_map/lay_by_head/pallas_call | solution.py:38
  1.8 11.6 %all-to-all-start = ((bf16[8,2,64,256]{3,2,1,0:T(8,128)(2,1)}), bf16[8,2,64,256]{3,2,1,0:T(8,128)(2,1)S(1)}, u32[]{:S(2)}, u32[]{:S(2)}) async-start(bf16[8,2,64,256]{3,2,1,0:T(8,128)(2,1)} %lay_by_head.1), calls=%async_computation | async-start | bytes 1048576 | tf_op jit(solution)/shard_map/all_to_all | solution.py:308
  13.7 0.2 select_reduce_fusion
  13.9 1.0 collective-permute-start
  14.9 0.8 collective-permute-done
  15.8 2.5 %collective-permute-start.3 = (s32[2,32]{1,0:T(2,128)S(1)}, s32[2,32]{1,0:T(2,128)S(1)}, u32[]{:S(2)}, u32[]{:S(2)}) collective-permute-start(s32[2,32]{1,0:T(2,128)S(1)} %pad_add_fusion), channel_id=1, source_target_pairs={{0,48},{8,56},{16,32},{24,40},{32,16},{40,24},{48,0},{56,8},{64,11... | collective-permute-start | bytes 776 | tf_op jit(solution)/shard_map/ppermute | solution.py:284
  18.2 0.5 collective-permute-start.2
  18.8 0.3 collective-permute-start.1
  19.0 0.7 collective-permute-done.3
  19.7 2.8 %collective-permute-done.2 = s32[2,32]{1,0:T(2,128)S(1)} collective-permute-done((s32[2,32]{1,0:T(2,128)S(1)}, s32[2,32]{1,0:T(2,128)S(1)}, u32[]{:S(2)}, u32[]{:S(2)}) %collective-permute-start.2) | collective-permute-done | bytes 288 | tf_op jit(solution)/shard_map/ppermute | solution.py:284
  22.5 1.7 %collective-permute-start.6 = (s32[8,32]{1,0:T(8,128)S(1)}, s32[8,32]{1,0:T(8,128)S(1)}, u32[]{:S(2)}, u32[]{:S(2)}) collective-permute-start(s32[8,32]{1,0:T(8,128)S(1)} %concatenate.12), channel_id=1, source_target_pairs={{0,192},{8,200},{16,208},{24,216},{32,224},{40,232},{48,240},{56,2... | collective-permute-start | bytes 3080 | tf_op jit(solution)/shard_map/ppermute | solution.py:284
  24.2 1.9 %collective-permute-start.4 = (s32[8,32]{1,0:T(8,128)S(1)}, s32[8,32]{1,0:T(8,128)S(1)}, u32[]{:S(2)}, u32[]{:S(2)}) collective-permute-start(s32[8,32]{1,0:T(8,128)S(1)} %concatenate.12), channel_id=1, source_target_pairs={{0,64},{8,72},{16,80},{24,88},{32,96},{40,104},{48,112},{56,120},{... | collective-permute-start | bytes 3080 | tf_op jit(solution)/shard_map/ppermute | solution.py:284
  26.1 1.0 collective-permute-done.6
  27.1 0.7 collective-permute-done.5
  27.9 0.1 select_reduce_fusion.2
  28.0 0.1 copy.10
  28.1 0.1 reshape.154.wanted_ref
  28.2 1.9 %pick_blocks.1 = bf16[64,64,256]{2,1,0:T(8,128)(2,1)} custom-call(s32[64]{0:T(128)S(1)} %reshape.154.wanted_ref, s32[1]{0:T(128)} %bitcast.3.me_ref, bf16[16,64,256]{2,1,0:T(8,128)(2,1)S(1)} %bitcast.8), custom_call_target="tpu_custom_call" | custom-call | tf_op jit(solution)/shard_map/pick_blocks/pallas_call | solution.py:69
  30.2 11.5 %all-to-all-start.1 = ((bf16[64,64,256]{2,1,0:T(8,128)(2,1)}), bf16[64,64,256]{2,1,0:T(8,128)(2,1)}, u32[]{:S(2)}, u32[]{:S(2)}) async-start(bf16[64,64,256]{2,1,0:T(8,128)(2,1)} %pick_blocks.1), calls=%async_computation.1 | async-start | bytes 4194304 | tf_op jit(solution)/shard_map/all_to_all | solution.py:311
  41.8 0.2 and_reduce_fusion
  42.0 13.8 %fresh_attention.1 = (f32[1024,1024]{1,0:T(8,128)}, f32[4,1024,128]{2,1,0:T(8,128)S(1)}, f32[4]{0:T(128)S(1)}) custom-call(s32[2]{0:T(128)S(1)} %copy-done.2, bf16[1024,1024]{1,0:T(8,128)(2,1)} %q_ref.3, bf16[1024,256]{1,0:T(8,128)(2,1)S(1)} %copy-done.1), custom_call_target="tpu_custom_call" | custom-call | flops 4294967296 | bytes 12582912 | tf_op jit(solution)/shard_map/fresh_attention/pallas_call | solution.py:126
  55.9 1.3 %copy-done.4 = f32[4,1024,128]{2,1,0:T(8,128)} copy-done((f32[4,1024,128]{2,1,0:T(8,128)}, f32[4,1024,128]{2,1,0:T(8,128)S(1)}, u32[]{:S(2)}) %copy-start.4) | copy-done | bytes 2097176
  57.2 32.6 %all-to-all-done.1.recv_any = bf16[64,64,256]{2,1,0:T(8,128)(2,1)} async-done(((bf16[64,64,256]{2,1,0:T(8,128)(2,1)}), bf16[64,64,256]{2,1,0:T(8,128)(2,1)}, u32[]{:S(2)}, u32[]{:S(2)}) %all-to-all-start.1) | async-done | bytes 2097184 | tf_op jit(solution)/shard_map/all_to_all | solution.py:311
  89.9 18.6 %prefix_attention.1 = bf16[1024,1024]{1,0:T(8,128)(2,1)} custom-call(s32[2]{0:T(128)S(1)} %copy-done.2, s32[32]{0:T(128)S(1)} %add_select_fusion.place_ref, s32[2]{0:T(128)S(1)} %copy-done.3, f32[4]{0:T(128)S(1)} %get-tuple-element.8.excess_ref, bf16[1024,1024]{1,0:T(8,128)(2,1)S(1)} %copy-done, bf16[64,64,256]{2,1,0:T(8,128)(2,1)} %all-to-all-done.1.recv_any, ...), custom_call_target="tpu_custom_call" | custom-call | flops 4294967296 | bytes 12582912 | tf_op jit(solution)/shard_map/prefix_attention/pallas_call | solution.py:249
  (30 shorter events, 0.5 us)
Async XLA Ops:
  0.0 13.5 %copy-start.3 = (s32[2]{0:T(128)S(1)}, s32[2]{0:T(128)}, u32[]{:S(2)}) copy-start(s32[2]{0:T(128)} %count_ref.1) | copy-start | bytes 28
  0.0 13.6 %copy-start.6 = (s32[2,16]{1,0:T(2,128)S(1)}, s32[2,16]{1,0:T(2,128)}, u32[]{:S(2)}) copy-start(s32[2,16]{1,0:T(2,128)} %param.11) | copy-start | bytes 388
  0.0 13.7 %copy-start.5 = (s32[512]{0:T(512)S(1)}, s32[512]{0:T(512)}, u32[]{:S(2)}) copy-start(s32[512]{0:T(512)} %param.13) | copy-start | bytes 6148
  1.8 26.4 %all-to-all-start = ((bf16[8,2,64,256]{3,2,1,0:T(8,128)(2,1)}), bf16[8,2,64,256]{3,2,1,0:T(8,128)(2,1)S(1)}, u32[]{:S(2)}, u32[]{:S(2)}) async-start(bf16[8,2,64,256]{3,2,1,0:T(8,128)(2,1)} %lay_by_head.1), calls=%async_computation | async-start | bytes 1048576 | tf_op jit(solution)/shard_map/all_to_all | solution.py:308
  13.9 1.9 %collective-permute-start = (s32[1,32]{1,0:T(1,128)S(1)}, s32[1,32]{1,0:T(1,128)S(1)}, u32[]{:S(2)}, u32[]{:S(2)}) collective-permute-start(s32[1,32]{1,0:T(1,128)S(1)} %bitcast_select_fusion), channel_id=1, source_target_pairs={{0,8},{8,0},{16,24},{24,16},{32,40},{40,32},{48,56},{56,48},{64,72... | collective-permute-start | bytes 392 | tf_op jit(solution)/shard_map/ppermute | solution.py:284
  15.8 3.9 %collective-permute-start.3 = (s32[2,32]{1,0:T(2,128)S(1)}, s32[2,32]{1,0:T(2,128)S(1)}, u32[]{:S(2)}, u32[]{:S(2)}) collective-permute-start(s32[2,32]{1,0:T(2,128)S(1)} %pad_add_fusion), channel_id=1, source_target_pairs={{0,48},{8,56},{16,32},{24,40},{32,16},{40,24},{48,0},{56,8},{64,11... | collective-permute-start | bytes 776 | tf_op jit(solution)/shard_map/ppermute | solution.py:284
  18.2 4.2 %collective-permute-start.2 = (s32[2,32]{1,0:T(2,128)S(1)}, s32[2,32]{1,0:T(2,128)S(1)}, u32[]{:S(2)}, u32[]{:S(2)}) collective-permute-start(s32[2,32]{1,0:T(2,128)S(1)} %pad_add_fusion), channel_id=1, source_target_pairs={{0,32},{8,40},{16,48},{24,56},{32,0},{40,8},{48,16},{56,24},{64,96... | collective-permute-start | bytes 776 | tf_op jit(solution)/shard_map/ppermute | solution.py:284
  18.8 3.7 %collective-permute-start.1 = (s32[2,32]{1,0:T(2,128)S(1)}, s32[2,32]{1,0:T(2,128)S(1)}, u32[]{:S(2)}, u32[]{:S(2)}) collective-permute-start(s32[2,32]{1,0:T(2,128)S(1)} %pad_add_fusion), channel_id=1, source_target_pairs={{0,16},{8,24},{16,0},{24,8},{32,48},{40,56},{48,32},{56,40},{64,80... | collective-permute-start | bytes 776 | tf_op jit(solution)/shard_map/ppermute | solution.py:284
  22.5 4.6 %collective-permute-start.6 = (s32[8,32]{1,0:T(8,128)S(1)}, s32[8,32]{1,0:T(8,128)S(1)}, u32[]{:S(2)}, u32[]{:S(2)}) collective-permute-start(s32[8,32]{1,0:T(8,128)S(1)} %concatenate.12), channel_id=1, source_target_pairs={{0,192},{8,200},{16,208},{24,216},{32,224},{40,232},{48,240},{56,2... | collective-permute-start | bytes 3080 | tf_op jit(solution)/shard_map/ppermute | solution.py:284
  24.2 3.7 %collective-permute-start.5 = (s32[8,32]{1,0:T(8,128)S(1)}, s32[8,32]{1,0:T(8,128)S(1)}, u32[]{:S(2)}, u32[]{:S(2)}) collective-permute-start(s32[8,32]{1,0:T(8,128)S(1)} %concatenate.12), channel_id=1, source_target_pairs={{0,128},{8,136},{16,144},{24,152},{32,160},{40,168},{48,176},{56,1... | collective-permute-start | bytes 3080 | tf_op jit(solution)/shard_map/ppermute | solution.py:284
  24.2 3.7 %collective-permute-start.4 = (s32[8,32]{1,0:T(8,128)S(1)}, s32[8,32]{1,0:T(8,128)S(1)}, u32[]{:S(2)}, u32[]{:S(2)}) collective-permute-start(s32[8,32]{1,0:T(8,128)S(1)} %concatenate.12), channel_id=1, source_target_pairs={{0,64},{8,72},{16,80},{24,88},{32,96},{40,104},{48,112},{56,120},{... | collective-permute-start | bytes 3080 | tf_op jit(solution)/shard_map/ppermute | solution.py:284
  30.2 11.8 %copy-start.1 = (bf16[1024,256]{1,0:T(8,128)(2,1)S(1)}, bf16[1024,256]{1,0:T(8,128)(2,1)}, u32[]{:S(2)}) copy-start(bf16[1024,256]{1,0:T(8,128)(2,1)} %kv_ref.1) | copy-start | bytes 1572868
  30.2 11.8 %copy-start.2 = (s32[2]{0:T(128)S(1)}, s32[2]{0:T(128)}, u32[]{:S(2)}) copy-start(s32[2]{0:T(128)} %owner_ref.3) | copy-start | bytes 28
  30.2 59.6 %all-to-all-start.1 = ((bf16[64,64,256]{2,1,0:T(8,128)(2,1)}), bf16[64,64,256]{2,1,0:T(8,128)(2,1)}, u32[]{:S(2)}, u32[]{:S(2)}) async-start(bf16[64,64,256]{2,1,0:T(8,128)(2,1)} %pick_blocks.1), calls=%async_computation.1 | async-start | bytes 4194304 | tf_op jit(solution)/shard_map/all_to_all | solution.py:311
  42.0 47.9 %copy-start = (bf16[1024,1024]{1,0:T(8,128)(2,1)S(1)}, bf16[1024,1024]{1,0:T(8,128)(2,1)}, u32[]{:S(2)}) copy-start(bf16[1024,1024]{1,0:T(8,128)(2,1)} %q_ref.3) | copy-start | bytes 6291460
  55.9 1.3 %copy-start.4 = (f32[4,1024,128]{2,1,0:T(8,128)}, f32[4,1024,128]{2,1,0:T(8,128)S(1)}, u32[]{:S(2)}) copy-start(f32[4,1024,128]{2,1,0:T(8,128)S(1)} %get-tuple-element.10.stat_any) | copy-start | bytes 6291460

commit v7 on v6

--- a/solution.py
+++ b/solution.py
@@ -14,7 +14,7 @@
 PB = 64
 SLOT_CAP = 2
 MIN_LIVE = 12
-PICK_STEP = 4
+PICK_STEP = 8
 ROW_TILE = 256
 EXP_SCALE = math.log2(math.e) / math.sqrt(HD)
 MASKED = -1e30

time: 109 us -> 109 us (level)
  no operation moved by 1% of the time
where the time goes in v7:
time: 109 us
  waiting for transfers between devices  38.7 us (36%)
  Pallas kernels  36.1 us (33%)
  starting transfers between devices  31 us (28%)
  local copies, waits for them, and re-layouts  1.87 us (2%)
    all_to_all x1, waiting for transfers between devices, on_device(): lax.all_to_all(to_send, 'req', split_axis=0, concat_axis=0, tiled=True)  32.6 us
    pallas_call x1, Pallas kernels, prefix_attention(): pl.pallas_call(kernel, in_specs=[smem] * 4 + [pl.BlockSpec(memory_space=p...  18.6 us
    pallas_call x1, Pallas kernels, fresh_attention(): pl.pallas_call(kernel, grid_spec=pltpu.PrefetchScalarGridSpec(num_scalar_...  13.8 us
    all_to_all x1, starting transfers between devices, on_device(): lax.all_to_all(by_head, 'tp', split_axis=0, concat_axis=0, tiled=True)  11.6 us
    all_to_all x1, starting transfers between devices, on_device(): lax.all_to_all(to_send, 'req', split_axis=0, concat_axis=0, tiled=True)  11.5 us
    ppermute x7, starting transfers between devices, share_over_req(): lax.ppermute(known, 'req', [(d, d ^ step) for d in range(groups)])  7.92 us
    ppermute x7, waiting for transfers between devices, share_over_req(): lax.ppermute(known, 'req', [(d, d ^ step) for d in range(groups)])  6.01 us
  transfers between devices with their start and end apart: 9, of which 6 were waited for; matrix products, arithmetic and copies ran while one was open for 1% of the time, Pallas kernels for 13%

profile of v7, /device:TPU:1, one launch (start us, length us, event | category | flops | bytes accessed | tf_op | source)
XLA Modules:
  0.0 108.6 jit_solution(17850353293920845978)
XLA Ops:
  0.0 1.8 %lay_by_head.1 = bf16[8,2,64,256]{3,2,1,0:T(8,128)(2,1)} custom-call(bf16[2,64,2048]{2,1,0:T(8,128)(2,1)} %pool_ref.1), custom_call_target="tpu_custom_call" | custom-call | tf_op jit(solution)/shard_map/lay_by_head/pallas_call | solution.py:38
  1.8 11.6 %all-to-all-start = ((bf16[8,2,64,256]{3,2,1,0:T(8,128)(2,1)}), bf16[8,2,64,256]{3,2,1,0:T(8,128)(2,1)S(1)}, u32[]{:S(2)}, u32[]{:S(2)}) async-start(bf16[8,2,64,256]{3,2,1,0:T(8,128)(2,1)} %lay_by_head.1), calls=%async_computation | async-start | bytes 1048576 | tf_op jit(solution)/shard_map/all_to_all | solution.py:308
  13.7 0.2 select_reduce_fusion
  13.9 1.0 collective-permute-start
  14.9 0.8 collective-permute-done
  15.8 2.5 %collective-permute-start.3 = (s32[2,32]{1,0:T(2,128)S(1)}, s32[2,32]{1,0:T(2,128)S(1)}, u32[]{:S(2)}, u32[]{:S(2)}) collective-permute-start(s32[2,32]{1,0:T(2,128)S(1)} %pad_add_fusion), channel_id=1, source_target_pairs={{0,48},{8,56},{16,32},{24,40},{32,16},{40,24},{48,0},{56,8},{64,11... | collective-permute-start | bytes 776 | tf_op jit(solution)/shard_map/ppermute | solution.py:284
  18.2 0.5 collective-permute-start.2
  18.8 0.3 collective-permute-start.1
  19.0 0.7 collective-permute-done.3
  19.7 2.8 %collective-permute-done.2 = s32[2,32]{1,0:T(2,128)S(1)} collective-permute-done((s32[2,32]{1,0:T(2,128)S(1)}, s32[2,32]{1,0:T(2,128)S(1)}, u32[]{:S(2)}, u32[]{:S(2)}) %collective-permute-start.2) | collective-permute-done | bytes 288 | tf_op jit(solution)/shard_map/ppermute | solution.py:284
  22.5 1.7 %collective-permute-start.6 = (s32[8,32]{1,0:T(8,128)S(1)}, s32[8,32]{1,0:T(8,128)S(1)}, u32[]{:S(2)}, u32[]{:S(2)}) collective-permute-start(s32[8,32]{1,0:T(8,128)S(1)} %concatenate.12), channel_id=1, source_target_pairs={{0,192},{8,200},{16,208},{24,216},{32,224},{40,232},{48,240},{56,2... | collective-permute-start | bytes 3080 | tf_op jit(solution)/shard_map/ppermute | solution.py:284
  24.2 1.9 %collective-permute-start.4 = (s32[8,32]{1,0:T(8,128)S(1)}, s32[8,32]{1,0:T(8,128)S(1)}, u32[]{:S(2)}, u32[]{:S(2)}) collective-permute-start(s32[8,32]{1,0:T(8,128)S(1)} %concatenate.12), channel_id=1, source_target_pairs={{0,64},{8,72},{16,80},{24,88},{32,96},{40,104},{48,112},{56,120},{... | collective-permute-start | bytes 3080 | tf_op jit(solution)/shard_map/ppermute | solution.py:284
  26.1 1.0 collective-permute-done.6
  27.1 0.7 collective-permute-done.5
  27.9 0.1 select_reduce_fusion.2
  28.0 0.1 copy.10
  28.1 0.1 reshape.154.wanted_ref
  28.2 1.9 %pick_blocks.1 = bf16[64,64,256]{2,1,0:T(8,128)(2,1)} custom-call(s32[64]{0:T(128)S(1)} %reshape.154.wanted_ref, s32[1]{0:T(128)} %bitcast.3.me_ref, bf16[16,64,256]{2,1,0:T(8,128)(2,1)S(1)} %bitcast.8), custom_call_target="tpu_custom_call" | custom-call | tf_op jit(solution)/shard_map/pick_blocks/pallas_call | solution.py:69
  30.2 11.5 %all-to-all-start.1 = ((bf16[64,64,256]{2,1,0:T(8,128)(2,1)}), bf16[64,64,256]{2,1,0:T(8,128)(2,1)}, u32[]{:S(2)}, u32[]{:S(2)}) async-start(bf16[64,64,256]{2,1,0:T(8,128)(2,1)} %pick_blocks.1), calls=%async_computation.1 | async-start | bytes 4194304 | tf_op jit(solution)/shard_map/all_to_all | solution.py:311
  41.8 0.2 and_reduce_fusion
  42.0 13.8 %fresh_attention.1 = (f32[1024,1024]{1,0:T(8,128)}, f32[4,1024,128]{2,1,0:T(8,128)S(1)}, f32[4]{0:T(128)S(1)}) custom-call(s32[2]{0:T(128)S(1)} %copy-done.2, bf16[1024,1024]{1,0:T(8,128)(2,1)} %q_ref.3, bf16[1024,256]{1,0:T(8,128)(2,1)S(1)} %copy-done.1), custom_call_target="tpu_custom_call" | custom-call | flops 4294967296 | bytes 12582912 | tf_op jit(solution)/shard_map/fresh_attention/pallas_call | solution.py:126
  55.9 1.3 %copy-done.4 = f32[4,1024,128]{2,1,0:T(8,128)} copy-done((f32[4,1024,128]{2,1,0:T(8,128)}, f32[4,1024,128]{2,1,0:T(8,128)S(1)}, u32[]{:S(2)}) %copy-start.4) | copy-done | bytes 2097176
  57.2 32.6 %all-to-all-done.1.recv_any = bf16[64,64,256]{2,1,0:T(8,128)(2,1)} async-done(((bf16[64,64,256]{2,1,0:T(8,128)(2,1)}), bf16[64,64,256]{2,1,0:T(8,128)(2,1)}, u32[]{:S(2)}, u32[]{:S(2)}) %all-to-all-start.1) | async-done | bytes 2097184 | tf_op jit(solution)/shard_map/all_to_all | solution.py:311
  89.9 18.6 %prefix_attention.1 = bf16[1024,1024]{1,0:T(8,128)(2,1)} custom-call(s32[2]{0:T(128)S(1)} %copy-done.2, s32[32]{0:T(128)S(1)} %add_select_fusion.place_ref, s32[2]{0:T(128)S(1)} %copy-done.3, f32[4]{0:T(128)S(1)} %get-tuple-element.8.excess_ref, bf16[1024,1024]{1,0:T(8,128)(2,1)S(1)} %copy-done, bf16[64,64,256]{2,1,0:T(8,128)(2,1)} %all-to-all-done.1.recv_any, ...), custom_call_target="tpu_custom_call" | custom-call | flops 4294967296 | bytes 12582912 | tf_op jit(solution)/shard_map/prefix_attention/pallas_call | solution.py:249
  (30 shorter events, 0.5 us)
Async XLA Ops:
  0.0 13.5 %copy-start.3 = (s32[2]{0:T(128)S(1)}, s32[2]{0:T(128)}, u32[]{:S(2)}) copy-start(s32[2]{0:T(128)} %count_ref.1) | copy-start | bytes 28
  0.0 13.6 %copy-start.6 = (s32[2,16]{1,0:T(2,128)S(1)}, s32[2,16]{1,0:T(2,128)}, u32[]{:S(2)}) copy-start(s32[2,16]{1,0:T(2,128)} %param.11) | copy-start | bytes 388
  0.0 13.7 %copy-start.5 = (s32[512]{0:T(512)S(1)}, s32[512]{0:T(512)}, u32[]{:S(2)}) copy-start(s32[512]{0:T(512)} %param.13) | copy-start | bytes 6148
  1.8 26.4 %all-to-all-start = ((bf16[8,2,64,256]{3,2,1,0:T(8,128)(2,1)}), bf16[8,2,64,256]{3,2,1,0:T(8,128)(2,1)S(1)}, u32[]{:S(2)}, u32[]{:S(2)}) async-start(bf16[8,2,64,256]{3,2,1,0:T(8,128)(2,1)} %lay_by_head.1), calls=%async_computation | async-start | bytes 1048576 | tf_op jit(solution)/shard_map/all_to_all | solution.py:308
  13.9 1.9 %collective-permute-start = (s32[1,32]{1,0:T(1,128)S(1)}, s32[1,32]{1,0:T(1,128)S(1)}, u32[]{:S(2)}, u32[]{:S(2)}) collective-permute-start(s32[1,32]{1,0:T(1,128)S(1)} %bitcast_select_fusion), channel_id=1, source_target_pairs={{0,8},{8,0},{16,24},{24,16},{32,40},{40,32},{48,56},{56,48},{64,72... | collective-permute-start | bytes 392 | tf_op jit(solution)/shard_map/ppermute | solution.py:284
  15.8 3.9 %collective-permute-start.3 = (s32[2,32]{1,0:T(2,128)S(1)}, s32[2,32]{1,0:T(2,128)S(1)}, u32[]{:S(2)}, u32[]{:S(2)}) collective-permute-start(s32[2,32]{1,0:T(2,128)S(1)} %pad_add_fusion), channel_id=1, source_target_pairs={{0,48},{8,56},{16,32},{24,40},{32,16},{40,24},{48,0},{56,8},{64,11... | collective-permute-start | bytes 776 | tf_op jit(solution)/shard_map/ppermute | solution.py:284
  18.2 4.2 %collective-permute-start.2 = (s32[2,32]{1,0:T(2,128)S(1)}, s32[2,32]{1,0:T(2,128)S(1)}, u32[]{:S(2)}, u32[]{:S(2)}) collective-permute-start(s32[2,32]{1,0:T(2,128)S(1)} %pad_add_fusion), channel_id=1, source_target_pairs={{0,32},{8,40},{16,48},{24,56},{32,0},{40,8},{48,16},{56,24},{64,96... | collective-permute-start | bytes 776 | tf_op jit(solution)/shard_map/ppermute | solution.py:284
  18.8 3.7 %collective-permute-start.1 = (s32[2,32]{1,0:T(2,128)S(1)}, s32[2,32]{1,0:T(2,128)S(1)}, u32[]{:S(2)}, u32[]{:S(2)}) collective-permute-start(s32[2,32]{1,0:T(2,128)S(1)} %pad_add_fusion), channel_id=1, source_target_pairs={{0,16},{8,24},{16,0},{24,8},{32,48},{40,56},{48,32},{56,40},{64,80... | collective-permute-start | bytes 776 | tf_op jit(solution)/shard_map/ppermute | solution.py:284
  22.5 4.6 %collective-permute-start.6 = (s32[8,32]{1,0:T(8,128)S(1)}, s32[8,32]{1,0:T(8,128)S(1)}, u32[]{:S(2)}, u32[]{:S(2)}) collective-permute-start(s32[8,32]{1,0:T(8,128)S(1)} %concatenate.12), channel_id=1, source_target_pairs={{0,192},{8,200},{16,208},{24,216},{32,224},{40,232},{48,240},{56,2... | collective-permute-start | bytes 3080 | tf_op jit(solution)/shard_map/ppermute | solution.py:284
  24.2 3.7 %collective-permute-start.5 = (s32[8,32]{1,0:T(8,128)S(1)}, s32[8,32]{1,0:T(8,128)S(1)}, u32[]{:S(2)}, u32[]{:S(2)}) collective-permute-start(s32[8,32]{1,0:T(8,128)S(1)} %concatenate.12), channel_id=1, source_target_pairs={{0,128},{8,136},{16,144},{24,152},{32,160},{40,168},{48,176},{56,1... | collective-permute-start | bytes 3080 | tf_op jit(solution)/shard_map/ppermute | solution.py:284
  24.2 3.7 %collective-permute-start.4 = (s32[8,32]{1,0:T(8,128)S(1)}, s32[8,32]{1,0:T(8,128)S(1)}, u32[]{:S(2)}, u32[]{:S(2)}) collective-permute-start(s32[8,32]{1,0:T(8,128)S(1)} %concatenate.12), channel_id=1, source_target_pairs={{0,64},{8,72},{16,80},{24,88},{32,96},{40,104},{48,112},{56,120},{... | collective-permute-start | bytes 3080 | tf_op jit(solution)/shard_map/ppermute | solution.py:284
  30.2 11.8 %copy-start.1 = (bf16[1024,256]{1,0:T(8,128)(2,1)S(1)}, bf16[1024,256]{1,0:T(8,128)(2,1)}, u32[]{:S(2)}) copy-start(bf16[1024,256]{1,0:T(8,128)(2,1)} %kv_ref.1) | copy-start | bytes 1572868
  30.2 11.8 %copy-start.2 = (s32[2]{0:T(128)S(1)}, s32[2]{0:T(128)}, u32[]{:S(2)}) copy-start(s32[2]{0:T(128)} %owner_ref.3) | copy-start | bytes 28
  30.2 59.6 %all-to-all-start.1 = ((bf16[64,64,256]{2,1,0:T(8,128)(2,1)}), bf16[64,64,256]{2,1,0:T(8,128)(2,1)}, u32[]{:S(2)}, u32[]{:S(2)}) async-start(bf16[64,64,256]{2,1,0:T(8,128)(2,1)} %pick_blocks.1), calls=%async_computation.1 | async-start | bytes 4194304 | tf_op jit(solution)/shard_map/all_to_all | solution.py:311
  42.0 47.9 %copy-start = (bf16[1024,1024]{1,0:T(8,128)(2,1)S(1)}, bf16[1024,1024]{1,0:T(8,128)(2,1)}, u32[]{:S(2)}) copy-start(bf16[1024,1024]{1,0:T(8,128)(2,1)} %q_ref.3) | copy-start | bytes 6291460
  55.9 1.3 %copy-start.4 = (f32[4,1024,128]{2,1,0:T(8,128)}, f32[4,1024,128]{2,1,0:T(8,128)S(1)}, u32[]{:S(2)}) copy-start(f32[4,1024,128]{2,1,0:T(8,128)S(1)} %get-tuple-element.10.stat_any) | copy-start | bytes 6291460
